TPU v7x, 768 devices: a whole 4x8x12 slice. The times are simulated.
768 devices in a mesh: col: 24 (over z, core), row: 4 (over x), rep: 8 (over y).
Axes of the slice: x: 4, y: 8, z: 12, core: 2. Of those that a mesh axis runs over, the one named last changes fastest.
Arguments:
- pooled_grad: bfloat16 [32, 3072, 48, 256], P(('row', 'rep'), 'col'), may hold values from -6 to 6
- giant_slot: int32 [24, 32, 3072, 8], P('col', ('row', 'rep')), may hold values from 0 to 2047, as said below
- touched_rows: int32 [24, 32, 32, 64], P('col', None, ('row', 'rep')), may hold values from 0 to 512, as said below
- bag_lengths: int32 [24, 32, 3072, 2], P('col', ('row', 'rep')), may hold values from 1 to 8, as said below
- small_ids: int32 [24, 32, 3072, 8], P('col', ('row', 'rep')), may hold values from 0 to 1023
- giant_weight: float32 [24, 16384, 256], P('col', ('row', 'rep')), may hold values from -4 to 4
- giant_accum: float32 [24, 16384], P('col', ('row', 'rep')), may hold values from 0.1 to 10
- small_weight: float32 [24, 1024, 256], P('col'), may hold values from -4 to 4
- small_accum: float32 [24, 1024], P('col'), may hold values from 0.1 to 10
Outputs:
- new_giant_weight: float32 [24, 16384, 256], P('col', ('row', 'rep'))
- new_giant_accum: float32 [24, 16384], P('col', ('row', 'rep'))
- new_small_weight: float32 [24, 1024, 256], P('col')
- new_small_accum: float32 [24, 1024], P('col')
Inputs may be any that keep to these rules, and one draw needn't show every extreme that they name: touched_rows[c, s, d, :] holds local rows of shard d; its first entries are live and the rest equal 512; for each table one shard gets all 64 entries live from every source group, the block from group 0 to the last shard is full too, and every block has at least 16 live entries. giant_slot[c, s, j, k] = d * 64 + m names a live entry m of touched_rows[c, s, d, :]; the smallest and the largest value are taken in every draw. `bag_lengths`: in every sample group one sample uses all 8 positions for both tables.
All inputs are finite; a program needn't handle non-finite values.
Results may differ from a plain program's by a relative error of at most 0.0003.
Values may be sent and summed in bfloat16 or wider, within the bound.
No kernel may reach another device: no remote copies, remote signals or barrier semaphores. Data moves between devices by JAX's collectives and lax.ppermute only.
A program may use at most 64 MiB of HBM per device.

v0:
```python
import math

import jax
import jax.numpy as jnp
from jax import lax
from jax.sharding import PartitionSpec as P

LEARN = 0.5
TINY = 1e-08


def rowwise_adagrad(weight, accumulator, gradient):
    accumulator_new = accumulator + jnp.mean(gradient * gradient, axis=-1)
    weight_new = weight - LEARN * gradient / (jnp.sqrt(accumulator_new)[..., None] + TINY)
    return (weight_new, accumulator_new)


def one_hot_sum(values, row_ids, lengths, bucket_count):
    sample_count = values.shape[0]
    block = math.gcd(sample_count, 512)
    is_live = lax.broadcasted_iota(jnp.int32, row_ids.shape, 1) < lengths[:, None]
    target = jnp.where(is_live, row_ids, bucket_count)
    target_blocks = target.reshape(sample_count // block, block, row_ids.shape[1])
    value_blocks = values.reshape(sample_count // block, block, values.shape[1])
    columns = lax.broadcasted_iota(jnp.int32, (1, bucket_count), 1)

    def add_block(total, block_inputs):
        block_target, block_values = block_inputs
        counts = jnp.zeros((block, bucket_count), jnp.bfloat16)
        for position in range(block_target.shape[1]):
            counts = counts + (block_target[:, position][:, None] == columns).astype(jnp.bfloat16)
        product = lax.dot_general(
            counts, block_values, (((0,), (0,)), ((), ())), preferred_element_type=jnp.float32
        )
        return (total + product, None)

    initial = jnp.zeros((bucket_count, values.shape[1]), jnp.float32)
    total, _ = lax.scan(add_block, initial, (target_blocks, value_blocks))
    return total


def body(
    pooled_grad,
    giant_slot,
    touched_rows,
    bag_lengths,
    small_ids,
    giant_weight,
    giant_accum,
    small_weight,
    small_accum,
):
    row_size = lax.axis_size("row")
    rep_size = lax.axis_size("rep")
    groups = row_size * rep_size
    capacity = touched_rows.shape[3]
    width = small_weight.shape[2]
    owned_grads = lax.all_to_all(pooled_grad, "col", split_axis=2, concat_axis=1, tiled=True)
    giant_values = owned_grads[0, :, 0, :]
    small_values = owned_grads[0, :, 1, :]
    lengths = bag_lengths[0, 0]
    slot_grad = one_hot_sum(giant_values, giant_slot[0, 0], lengths[:, 0], groups * capacity)
    blocks = slot_grad.reshape(groups, capacity, width)
    arrived = lax.all_to_all(blocks, ("row", "rep"), split_axis=0, concat_axis=0, tiled=True)
    small_grad = one_hot_sum(small_values, small_ids[0, 0], lengths[:, 1], small_weight.shape[1])
    row_targets = touched_rows[0, :, 0, :].reshape(-1)
    empty = jnp.zeros((giant_weight.shape[1], width), jnp.float32)
    giant_grad = empty.at[row_targets].add(arrived.reshape(-1, width), mode="drop")
    new_gw, new_ga = rowwise_adagrad(giant_weight[0], giant_accum[0], giant_grad)
    summed = lax.psum(small_grad, ("row", "rep"))
    new_sw, new_sa = rowwise_adagrad(small_weight[0], small_accum[0], summed)
    return (new_gw[None], new_ga[None], new_sw[None], new_sa[None])


def solution(mesh):
    placed = (
        P(("row", "rep"), "col", None, None),
        P("col", ("row", "rep"), None, None),
        P("col", None, ("row", "rep"), None),
        P("col", ("row", "rep"), None, None),
        P("col", ("row", "rep"), None, None),
        P("col", ("row", "rep"), None),
        P("col", ("row", "rep")),
        P("col", None, None),
        P("col", None),
    )
    return jax.shard_map(
        body,
        mesh=mesh,
        in_specs=placed,
        out_specs=(
            P("col", ("row", "rep"), None),
            P("col", ("row", "rep")),
            P("col", None, None),
            P("col", None),
        ),
        check_vma=False,
    )
```

profile of v0, /device:TPU:64, one launch (start us, length us, event | category | flops | bytes accessed | tf_op | source)
XLA Modules:
  0.0 404.6 jit_solution(13518623683849556141)
XLA Ops:
  7.2 4.6 %copy.16 = bf16[1,128,48,256]{3,1,0,2:T(8,128)(2,1)} copy(bf16[1,128,48,256]{3,2,1,0:T(8,128)(2,1)} %param.13) | data formatting | bytes 6291456 | tf_op args[0]
  11.8 0.0 copy-start.5
  11.8 0.0 copy-start.3
  11.8 0.0 copy-start.4
  11.8 15.0 %all-to-all-start = ((bf16[1,128,48,256]{3,1,0,2:T(8,128)(2,1)}), bf16[1,128,48,256]{3,1,0,2:T(8,128)(2,1)S(1)}, u32[]{:S(2)}, u32[]{:S(2)}) async-start(bf16[1,128,48,256]{3,1,0,2:T(8,128)(2,1)} %copy.16), calls=%async_computation | async-start | bytes 6291456 | tf_op jit(solution)/shard_map/all_to_all | solution.py:58
  26.8 0.0 copy-done.5
  26.8 0.1 slice_reduce_fusion
  26.9 0.0 copy-done.3
  27.0 0.0 copy-done.4
  27.0 103.5 %all-to-all-done = bf16[1,128,48,256]{3,1,0,2:T(8,128)(2,1)S(1)} async-done(((bf16[1,128,48,256]{3,1,0,2:T(8,128)(2,1)}), bf16[1,128,48,256]{3,1,0,2:T(8,128)(2,1)S(1)}, u32[]{:S(2)}, u32[]{:S(2)}) %all-to-all-start) | async-done | bytes 3145760 | tf_op jit(solution)/shard_map/all_to_all | solution.py:58
  130.5 0.2 copy.17
  130.7 0.0 copy-start
  130.7 1.9 fusion.80
  132.6 0.7 copy-done
  133.3 34.9 %while.24 = (s32[]{:T(128)}, f32[2048,256]{1,0:T(8,128)S(1)}, s32[6,512,8]{1,2,0:T(8,128)S(1)}, bf16[6,512,256]{2,1,0:T(8,128)(2,1)}, s32[]{:T(128)}, /*index=5*/s32[]{:T(128)}) while((s32[]{:T(128)}, f32[2048,256]{1,0:T(8,128)S(1)}, s32[6,512,8]{1,2,0:T(8,128)S(1)}, bf16[6,512,256]{2,1,0:T(8,128)(2,1)}, s32[]{:T(128)}, ...), condition=%wide.region_1.2_spmd.clone.clone, body=%wide.region_0.1_spmd.clone.clone.sunk | while | flops 571473920 | bytes 4538963 | solution.py:38
  133.3 5.8 %convolution_add_fusion.4 = f32[2048,256]{1,0:T(8,128)S(1)} fusion(f32[2048,256]{1,0:T(8,128)S(1)} %get-tuple-element.305, s32[512]{0:T(512)S(1)} %bitcast.103, s32[512]{0:T(512)S(1)} %bitcast.104, s32[512]{0:T(512)S(1)} %bitcast.105, s32[512]{0:T(512)S(1)} %bitcast.106, s32[512]{0:T(512)S(1)} %bitcast.107, s32[512]{0:T(512)S(1)} %bitcast.108, ...), kind=kOutput, calls=%fused_computation.19.clone.1 | convolution fusion | flops 571473920 | bytes 4473345 | tf_op jit(solution)/shard_map/while/body/eval_jaxpr/dot_general | solution.py:32
  139.1 5.7 %convolution_add_fusion.4 = f32[2048,256]{1,0:T(8,128)S(1)} fusion(f32[2048,256]{1,0:T(8,128)S(1)} %get-tuple-element.305, s32[512]{0:T(512)S(1)} %bitcast.103, s32[512]{0:T(512)S(1)} %bitcast.104, s32[512]{0:T(512)S(1)} %bitcast.105, s32[512]{0:T(512)S(1)} %bitcast.106, s32[512]{0:T(512)S(1)} %bitcast.107, s32[512]{0:T(512)S(1)} %bitcast.108, ...), kind=kOutput, calls=%fused_computation.19.clone.1 | convolution fusion | flops 571473920 | bytes 4473345 | tf_op jit(solution)/shard_map/while/body/eval_jaxpr/dot_general | solution.py:32
  144.9 5.8 %convolution_add_fusion.4 = f32[2048,256]{1,0:T(8,128)S(1)} fusion(f32[2048,256]{1,0:T(8,128)S(1)} %get-tuple-element.305, s32[512]{0:T(512)S(1)} %bitcast.103, s32[512]{0:T(512)S(1)} %bitcast.104, s32[512]{0:T(512)S(1)} %bitcast.105, s32[512]{0:T(512)S(1)} %bitcast.106, s32[512]{0:T(512)S(1)} %bitcast.107, s32[512]{0:T(512)S(1)} %bitcast.108, ...), kind=kOutput, calls=%fused_computation.19.clone.1 | convolution fusion | flops 571473920 | bytes 4473345 | tf_op jit(solution)/shard_map/while/body/eval_jaxpr/dot_general | solution.py:32
  150.7 5.7 %convolution_add_fusion.4 = f32[2048,256]{1,0:T(8,128)S(1)} fusion(f32[2048,256]{1,0:T(8,128)S(1)} %get-tuple-element.305, s32[512]{0:T(512)S(1)} %bitcast.103, s32[512]{0:T(512)S(1)} %bitcast.104, s32[512]{0:T(512)S(1)} %bitcast.105, s32[512]{0:T(512)S(1)} %bitcast.106, s32[512]{0:T(512)S(1)} %bitcast.107, s32[512]{0:T(512)S(1)} %bitcast.108, ...), kind=kOutput, calls=%fused_computation.19.clone.1 | convolution fusion | flops 571473920 | bytes 4473345 | tf_op jit(solution)/shard_map/while/body/eval_jaxpr/dot_general | solution.py:32
  156.6 5.8 %convolution_add_fusion.4 = f32[2048,256]{1,0:T(8,128)S(1)} fusion(f32[2048,256]{1,0:T(8,128)S(1)} %get-tuple-element.305, s32[512]{0:T(512)S(1)} %bitcast.103, s32[512]{0:T(512)S(1)} %bitcast.104, s32[512]{0:T(512)S(1)} %bitcast.105, s32[512]{0:T(512)S(1)} %bitcast.106, s32[512]{0:T(512)S(1)} %bitcast.107, s32[512]{0:T(512)S(1)} %bitcast.108, ...), kind=kOutput, calls=%fused_computation.19.clone.1 | convolution fusion | flops 571473920 | bytes 4473345 | tf_op jit(solution)/shard_map/while/body/eval_jaxpr/dot_general | solution.py:32
  162.4 5.7 %convolution_add_fusion.4 = f32[2048,256]{1,0:T(8,128)S(1)} fusion(f32[2048,256]{1,0:T(8,128)S(1)} %get-tuple-element.305, s32[512]{0:T(512)S(1)} %bitcast.103, s32[512]{0:T(512)S(1)} %bitcast.104, s32[512]{0:T(512)S(1)} %bitcast.105, s32[512]{0:T(512)S(1)} %bitcast.106, s32[512]{0:T(512)S(1)} %bitcast.107, s32[512]{0:T(512)S(1)} %bitcast.108, ...), kind=kOutput, calls=%fused_computation.19.clone.1 | convolution fusion | flops 571473920 | bytes 4473345 | tf_op jit(solution)/shard_map/while/body/eval_jaxpr/dot_general | solution.py:32
  168.1 0.0 copy-start.1
  168.1 1.3 copy-done.1
  169.5 9.9 %all-to-all-start.1 = ((f32[32,64,256]{2,1,0:T(8,128)}), f32[32,64,256]{2,1,0:T(8,128)S(1)}, u32[]{:S(2)}, u32[]{:S(2)}) async-start(f32[32,64,256]{2,1,0:T(8,128)} %bitcast.97), calls=%async_computation.1 | async-start | bytes 4194304 | tf_op jit(solution)/shard_map/all_to_all | solution.py:64
  179.4 0.2 all-reduce.2.cloned.1.call-start
  179.7 0.0 copy-start.6
  179.7 27.8 %while.25 = (s32[]{:T(128)}, f32[1024,256]{1,0:T(8,128)}, s32[6,512,8]{1,2,0:T(8,128)S(1)}, bf16[6,512,256]{2,1,0:T(8,128)(2,1)}, s32[]{:T(128)}, /*index=5*/s32[]{:T(128)}) while((s32[]{:T(128)}, f32[1024,256]{1,0:T(8,128)}, s32[6,512,8]{1,2,0:T(8,128)S(1)}, bf16[6,512,256]{2,1,0:T(8,128)(2,1)}, s32[]{:T(128)}, ...), condition=%wide.region_5.6_spmd.clone.clone, body=%wide.region_4.5_spmd.clone.clone.sunk | while | flops 285736960 | bytes 2441811 | solution.py:38
  179.7 4.3 %convolution_add_fusion.5 = f32[1024,256]{1,0:T(8,128)} fusion(f32[1024,256]{1,0:T(8,128)} %get-tuple-element.323, s32[512]{0:T(512)S(1)} %bitcast.111, s32[512]{0:T(512)S(1)} %bitcast.112, s32[512]{0:T(512)S(1)} %bitcast.113, s32[512]{0:T(512)S(1)} %bitcast.114, s32[512]{0:T(512)S(1)} %bitcast.115, s32[512]{0:T(512)S(1)} %bitcast.116, ...), kind=kOutput, calls=%fused_computation.55.clone.1 | convolution fusion | flops 285736960 | bytes 2376193 | tf_op jit(solution)/shard_map/while/body/eval_jaxpr/dot_general | solution.py:32
  184.0 4.7 %convolution_add_fusion.5 = f32[1024,256]{1,0:T(8,128)} fusion(f32[1024,256]{1,0:T(8,128)} %get-tuple-element.323, s32[512]{0:T(512)S(1)} %bitcast.111, s32[512]{0:T(512)S(1)} %bitcast.112, s32[512]{0:T(512)S(1)} %bitcast.113, s32[512]{0:T(512)S(1)} %bitcast.114, s32[512]{0:T(512)S(1)} %bitcast.115, s32[512]{0:T(512)S(1)} %bitcast.116, ...), kind=kOutput, calls=%fused_computation.55.clone.1 | convolution fusion | flops 285736960 | bytes 2376193 | tf_op jit(solution)/shard_map/while/body/eval_jaxpr/dot_general | solution.py:32
  188.7 4.7 %convolution_add_fusion.5 = f32[1024,256]{1,0:T(8,128)} fusion(f32[1024,256]{1,0:T(8,128)} %get-tuple-element.323, s32[512]{0:T(512)S(1)} %bitcast.111, s32[512]{0:T(512)S(1)} %bitcast.112, s32[512]{0:T(512)S(1)} %bitcast.113, s32[512]{0:T(512)S(1)} %bitcast.114, s32[512]{0:T(512)S(1)} %bitcast.115, s32[512]{0:T(512)S(1)} %bitcast.116, ...), kind=kOutput, calls=%fused_computation.55.clone.1 | convolution fusion | flops 285736960 | bytes 2376193 | tf_op jit(solution)/shard_map/while/body/eval_jaxpr/dot_general | solution.py:32
  193.4 4.7 %convolution_add_fusion.5 = f32[1024,256]{1,0:T(8,128)} fusion(f32[1024,256]{1,0:T(8,128)} %get-tuple-element.323, s32[512]{0:T(512)S(1)} %bitcast.111, s32[512]{0:T(512)S(1)} %bitcast.112, s32[512]{0:T(512)S(1)} %bitcast.113, s32[512]{0:T(512)S(1)} %bitcast.114, s32[512]{0:T(512)S(1)} %bitcast.115, s32[512]{0:T(512)S(1)} %bitcast.116, ...), kind=kOutput, calls=%fused_computation.55.clone.1 | convolution fusion | flops 285736960 | bytes 2376193 | tf_op jit(solution)/shard_map/while/body/eval_jaxpr/dot_general | solution.py:32
  198.1 4.7 %convolution_add_fusion.5 = f32[1024,256]{1,0:T(8,128)} fusion(f32[1024,256]{1,0:T(8,128)} %get-tuple-element.323, s32[512]{0:T(512)S(1)} %bitcast.111, s32[512]{0:T(512)S(1)} %bitcast.112, s32[512]{0:T(512)S(1)} %bitcast.113, s32[512]{0:T(512)S(1)} %bitcast.114, s32[512]{0:T(512)S(1)} %bitcast.115, s32[512]{0:T(512)S(1)} %bitcast.116, ...), kind=kOutput, calls=%fused_computation.55.clone.1 | convolution fusion | flops 285736960 | bytes 2376193 | tf_op jit(solution)/shard_map/while/body/eval_jaxpr/dot_general | solution.py:32
  202.8 4.7 %convolution_add_fusion.5 = f32[1024,256]{1,0:T(8,128)} fusion(f32[1024,256]{1,0:T(8,128)} %get-tuple-element.323, s32[512]{0:T(512)S(1)} %bitcast.111, s32[512]{0:T(512)S(1)} %bitcast.112, s32[512]{0:T(512)S(1)} %bitcast.113, s32[512]{0:T(512)S(1)} %bitcast.114, s32[512]{0:T(512)S(1)} %bitcast.115, s32[512]{0:T(512)S(1)} %bitcast.116, ...), kind=kOutput, calls=%fused_computation.55.clone.1 | convolution fusion | flops 285736960 | bytes 2376193 | tf_op jit(solution)/shard_map/while/body/eval_jaxpr/dot_general | solution.py:32
  207.4 0.0 copy-start.7
  207.4 0.0 copy-start.2
  207.4 0.0 all-reduce.2.cloned.1.call-update
  207.5 0.5 broadcast.79
  208.0 0.0 copy-done.6
  208.0 0.7 reduce.11
  208.7 0.1 reshape_squeeze.9
  208.8 170.1 %all-reduce.2.cloned.1.call-done = f32[1024,256]{1,0:T(8,128)} async-done(((f32[1024,256]{1,0:T(8,128)}), f32[1024,256]{1,0:T(8,128)}) %all-reduce.2.cloned.1.call-update) | async-done | bytes 1048592 | tf_op jit(solution)/shard_map/psum | solution.py:70
  378.8 1.4 multiply_reduce_fusion
  380.3 0.0 copy-done.7
  380.3 0.6 add.122
  380.9 0.0 copy-done.2
  380.9 0.0 copy-start.8
  380.9 2.4 fusion.72
  383.3 0.0 all-to-all-done.1
  383.3 11.7 %scatter_custom_fusion = f32[512,256]{1,0:T(8,128)S(1)} fusion(s32[2048]{0:T(1024)S(1)} %bitcast.121, f32[2048,256]{1,0:T(8,128)S(1)} %bitcast.96, f32[]{:T(128)} %constant.11.clone.1), kind=kCustom, calls=%fused_computation.81 | custom fusion | flops 524288 | bytes 524292 | tf_op jit(solution)/shard_map/scatter-add | solution.py:68
  395.0 0.1 multiply_reduce_fusion.1
  395.2 0.0 copy-done.8
  395.2 0.6 add.118
  395.8 2.0 fusion.73
  (33 shorter events, 0.3 us)
Async XLA Ops:
  11.8 15.0 %copy-start.5 = (s32[1,1,3072,2]{2,3,1,0:T(2,128)S(1)}, s32[1,1,3072,2]{2,3,1,0:T(2,128)}, u32[]{:S(2)}) copy-start(s32[1,1,3072,2]{2,3,1,0:T(2,128)} %param.16) | copy-start | bytes 73732
  11.8 15.1 %copy-start.3 = (s32[1,1,3072,8]{2,3,1,0:T(8,128)S(1)}, s32[1,1,3072,8]{2,3,1,0:T(8,128)}, u32[]{:S(2)}) copy-start(s32[1,1,3072,8]{2,3,1,0:T(8,128)} %param.17) | copy-start | bytes 294916
  11.8 15.1 %copy-start.4 = (s32[1,1,3072,8]{2,3,1,0:T(8,128)S(1)}, s32[1,1,3072,8]{2,3,1,0:T(8,128)}, u32[]{:S(2)}) copy-start(s32[1,1,3072,8]{2,3,1,0:T(8,128)} %param.14) | copy-start | bytes 294916
  11.8 118.7 %all-to-all-start = ((bf16[1,128,48,256]{3,1,0,2:T(8,128)(2,1)}), bf16[1,128,48,256]{3,1,0,2:T(8,128)(2,1)S(1)}, u32[]{:S(2)}, u32[]{:S(2)}) async-start(bf16[1,128,48,256]{3,1,0,2:T(8,128)(2,1)} %copy.16), calls=%async_computation | async-start | bytes 6291456 | tf_op jit(solution)/shard_map/all_to_all | solution.py:58
  130.7 2.6 copy-start
  168.1 1.3 copy-start.1
  169.5 213.9 %all-to-all-start.1 = ((f32[32,64,256]{2,1,0:T(8,128)}), f32[32,64,256]{2,1,0:T(8,128)S(1)}, u32[]{:S(2)}, u32[]{:S(2)}) async-start(f32[32,64,256]{2,1,0:T(8,128)} %bitcast.97), calls=%async_computation.1 | async-start | bytes 4194304 | tf_op jit(solution)/shard_map/all_to_all | solution.py:64
  179.4 199.4 %all-reduce.2.cloned.1.call-start = ((), (), s32[]{:S(2)}) async-start(), calls=%async_computation.2 | async-start | bytes 2097152 | tf_op jit(solution)/shard_map/psum | solution.py:70
  179.7 28.3 %copy-start.6 = (s32[1,32,1,64]{3,2,1,0:T(1,128)S(1)}, s32[1,32,1,64]{3,2,1,0:T(1,128)}, u32[]{:S(2)}) copy-start(s32[1,32,1,64]{3,2,1,0:T(1,128)} %param.15) | copy-start | bytes 24580
  207.4 172.8 %copy-start.7 = (f32[1,1024]{1,0:T(1,128)S(1)}, f32[1,1024]{1,0:T(1,128)}, u32[]{:S(2)}) copy-start(f32[1,1024]{1,0:T(1,128)} %param.21) | copy-start | bytes 12292
  207.4 173.5 %copy-start.2 = (f32[1,1024,256]{2,1,0:T(8,128)S(1)}, f32[1,1024,256]{2,1,0:T(8,128)}, u32[]{:S(2)}) copy-start(f32[1,1024,256]{2,1,0:T(8,128)} %param.20) | copy-start | bytes 3145732
  380.9 14.3 %copy-start.8 = (f32[1,512]{1,0:T(1,128)S(1)}, f32[1,512]{1,0:T(1,128)}, u32[]{:S(2)}) copy-start(f32[1,512]{1,0:T(1,128)} %param.19) | copy-start | bytes 6148
Sparse Core Ops, SparseCore 0:
  207.6 171.1 all-reduce.1
where the time goes:
time: 405 us
  waiting for transfers between devices  274 us (68%)
  matrix products  62.1 us (15%)
  starting transfers between devices  25.1 us (6%)
  other arithmetic  19.6 us (5%)
  between operations  14.2 us (4%)
  local copies, waits for them, and re-layouts  9.68 us (2%)
    psum x1, waiting for transfers between devices, body(): summed = lax.psum(small_grad, ('row', 'rep'))  170 us
    all_to_all x1, waiting for transfers between devices, body(): lax.all_to_all(pooled_grad, 'col', split_axis=2, concat_axis=1, tiled=True)  103 us
    dot_general x12, matrix products, add_block(): lax.dot_general(counts, block_values, (((0,), (0,)), ((), ())), preferred...  62.1 us
    all_to_all x1, starting transfers between devices, body(): lax.all_to_all(pooled_grad, 'col', split_axis=2, concat_axis=1, tiled=True)  15 us
    scatter-add x1, other arithmetic, body(): empty.at[row_targets].add(arrived.reshape(-1, width), mode='drop')  11.7 us
    all_to_all x1, starting transfers between devices, body(): lax.all_to_all(blocks, ('row', 'rep'), split_axis=0, concat_axis=0, tiled...  9.95 us
  transfers between devices with their start and end apart: 3, of which 2 were waited for; matrix products, arithmetic and copies ran while one was open for 8% of the time, Pallas kernels for 0%

commit v1 on v0

v1 whole, which is shorter than its diff:
```python
import functools

import jax
import jax.numpy as jnp
from jax import lax
from jax.experimental import pallas as pl
from jax.experimental.pallas import tpu as pltpu
from jax.sharding import PartitionSpec as P

LEARN = 0.5
TINY = 1e-08
BF = jnp.bfloat16
F32 = jnp.float32
VMEM_LIMIT = 48 * 1024 * 1024
TAG_ROWS = 16


def masked_ids(ids, lengths):
    live = lax.broadcasted_iota(jnp.int32, ids.shape, 1) < lengths[:, None]
    return jnp.where(live, ids, -1).T


def counts_kernel(ids_ref, out_ref):
    rows, samples = out_ref.shape
    bag = ids_ref.shape[0]
    lanes = 256
    first = pl.program_id(0) * rows
    local = lax.broadcasted_iota(jnp.int32, (16, lanes), 0)

    @pl.loop(0, samples // lanes)
    def _(chunk):
        at = pl.ds(pl.multiple_of(chunk * lanes, lanes), lanes)
        named = [jnp.broadcast_to(ids_ref[k : k + 1, at], (16, lanes)) for k in range(bag)]

        @pl.loop(0, rows // 16)
        def _(step):
            bucket = local + (first + step * 16)
            total = jnp.zeros((16, lanes), F32)
            for k in range(bag):
                total = total + jnp.where(named[k] == bucket, 1.0, 0.0)
            out_ref[pl.ds(pl.multiple_of(step * 16, 16), 16), at] = total.astype(BF)


def bag_counts(ids, buckets):
    bag, samples = ids.shape
    rows = 256
    return pl.pallas_call(
        counts_kernel,
        grid=(buckets // rows,),
        in_specs=[pl.BlockSpec((bag, samples), lambda i: (0, 0))],
        out_specs=pl.BlockSpec((rows, samples), lambda i: (i, 0)),
        out_shape=jax.ShapeDtypeStruct((buckets, samples), BF),
        compiler_params=pltpu.CompilerParams(vmem_limit_bytes=VMEM_LIMIT),
        cost_estimate=pl.CostEstimate(
            flops=3 * bag * buckets * samples, bytes_accessed=2 * buckets * samples, transcendentals=0
        ),
    )(ids)


def corner(array):
    lead = (1,) * (array.ndim - 2)
    return pl.BlockSpec(lead + (16, 128), lambda *_: (0,) * array.ndim)


def matmul_kernel(counts_ref, values_ref, left_ref, right_ref):
    sums = jnp.dot(counts_ref[...], values_ref[...], preferred_element_type=F32)
    half = left_ref.shape[1]
    left_ref[...] = sums[:, :half]
    right_ref[...] = sums[:, half:]


def packed_kernel(capacity, counts_ref, values_ref, later_ref, out_ref):
    del later_ref
    sums = jnp.dot(counts_ref[...], values_ref[...], preferred_element_type=F32)
    rows, width = sums.shape
    lanes = out_ref.shape[2]
    parts = width // lanes
    largest = jnp.maximum(jnp.max(jnp.abs(sums), axis=1, keepdims=True), 2.0**-100)
    power = jnp.floor(jnp.log2(largest) + 1e-3) - 14.0
    coded = jnp.round(sums * jnp.exp2(-power))
    coded = jnp.clip(coded, -32767.0, 32767.0).astype(jnp.int32).astype(jnp.int16)
    power = jnp.broadcast_to(power, (rows, lanes))
    for block in range(rows // capacity):
        mine = slice(block * capacity, (block + 1) * capacity)
        for part in range(parts):
            out_ref[block, part * capacity : (part + 1) * capacity, :] = coded[
                mine, part * lanes : (part + 1) * lanes
            ]
        tag = jnp.concatenate([power[mine, :], jnp.zeros((lanes - capacity, lanes), F32)], axis=0)
        out_ref[block, parts * capacity :, :] = tag.T[0:TAG_ROWS, :].astype(jnp.int32).astype(jnp.int16)


def bucket_sums(counts, values):
    buckets, samples = counts.shape
    width = values.shape[1]
    rows = 512
    return pl.pallas_call(
        matmul_kernel,
        grid=(buckets // rows,),
        in_specs=[
            pl.BlockSpec((rows, samples), lambda i: (i, 0)),
            pl.BlockSpec((samples, width), lambda i: (0, 0)),
        ],
        out_specs=[pl.BlockSpec((rows, width // 2), lambda i: (i, 0))] * 2,
        out_shape=[jax.ShapeDtypeStruct((buckets, width // 2), F32)] * 2,
        compiler_params=pltpu.CompilerParams(vmem_limit_bytes=VMEM_LIMIT),
    )(counts, values)


def packed_bucket_sums(counts, values, capacity, later):
    buckets, samples = counts.shape
    width = values.shape[1]
    rows, lanes = 512, 128
    tall = capacity * width // lanes + TAG_ROWS
    return pl.pallas_call(
        functools.partial(packed_kernel, capacity),
        grid=(buckets // rows,),
        in_specs=[
            pl.BlockSpec((rows, samples), lambda i: (i, 0)),
            pl.BlockSpec((samples, width), lambda i: (0, 0)),
            corner(later),
        ],
        out_specs=pl.BlockSpec((rows // capacity, tall, lanes), lambda i: (i, 0, 0)),
        out_shape=jax.ShapeDtypeStruct((buckets // capacity, tall, lanes), jnp.int16),
        compiler_params=pltpu.CompilerParams(vmem_limit_bytes=VMEM_LIMIT),
    )(counts, values, later)


def adagrad_step(weight_ref, accum_ref, grad, new_weight_ref, new_accum_ref):
    rows, width = grad.shape
    accum = jnp.broadcast_to(accum_ref[...], (8, rows)).T[:, 0:1]
    total = accum + jnp.sum(grad * grad, axis=1, keepdims=True) * (1.0 / width)
    new_weight_ref[...] = weight_ref[...] - grad * (LEARN / (jnp.sqrt(total) + TINY))
    new_accum_ref[...] = jnp.broadcast_to(total, (rows, 128)).T[0:1, :]


def giant_kernel(capacity, targets_ref, arrived_ref, weight_ref, accum_ref, new_weight_ref, new_accum_ref, parts):
    rows, width = weight_ref.shape
    groups, tall, lanes = arrived_ref.shape

    @pl.when(pl.program_id(0) == 0)
    def _():
        for group in range(groups):
            here = slice(group * capacity, (group + 1) * capacity)
            tag = arrived_ref[group, tall - TAG_ROWS :, :].astype(jnp.int32).astype(F32)
            scale = jnp.exp2(tag.T[0:capacity, 0:1])
            for part in range(width // lanes):
                value = arrived_ref[group, part * capacity : (part + 1) * capacity, :]
                value = value.astype(jnp.int32).astype(F32) * scale
                high = value.astype(BF)
                rest = value - high.astype(F32)
                middle = rest.astype(BF)
                low = (rest - middle.astype(F32)).astype(BF)
                for place, piece in enumerate((high, middle, low)):
                    at = place * width + part * lanes
                    parts[here, at : at + lanes] = piece

    sources = groups * capacity
    row = lax.broadcasted_iota(jnp.int32, (rows, sources), 0) + pl.program_id(0) * rows
    hit = jnp.where(jnp.broadcast_to(targets_ref[...], (rows, sources)) == row, 1.0, 0.0).astype(BF)
    product = jnp.dot(hit, parts[...], preferred_element_type=F32)
    grad = product[:, 0:width] + (product[:, width : 2 * width] + product[:, 2 * width :])
    adagrad_step(weight_ref, accum_ref, grad, new_weight_ref, new_accum_ref)


def giant_update(targets, arrived, weight, accum, capacity):
    total, width = weight.shape
    sources = targets.shape[1]
    rows = 256
    return pl.pallas_call(
        functools.partial(giant_kernel, capacity),
        grid=(total // rows,),
        in_specs=[
            pl.BlockSpec((1, sources), lambda i: (0, 0)),
            pl.BlockSpec(arrived.shape, lambda i: (0, 0, 0)),
            pl.BlockSpec((rows, width), lambda i: (i, 0)),
            pl.BlockSpec((1, rows), lambda i: (0, i)),
        ],
        out_specs=[
            pl.BlockSpec((rows, width), lambda i: (i, 0)),
            pl.BlockSpec((1, rows), lambda i: (0, i)),
        ],
        out_shape=[
            jax.ShapeDtypeStruct((total, width), F32),
            jax.ShapeDtypeStruct((1, total), F32),
        ],
        scratch_shapes=[pltpu.VMEM((sources, 3 * width), BF)],
        compiler_params=pltpu.CompilerParams(vmem_limit_bytes=VMEM_LIMIT),
    )(targets, arrived, weight, accum)


def small_kernel(left_ref, right_ref, weight_ref, accum_ref, new_weight_ref, new_accum_ref):
    grad = jnp.concatenate([left_ref[...], right_ref[...]], axis=1)
    adagrad_step(weight_ref, accum_ref, grad, new_weight_ref, new_accum_ref)


def small_update(left, right, weight, accum):
    total, width = weight.shape
    rows = 512
    half = pl.BlockSpec((rows, width // 2), lambda i: (i, 0))
    block = pl.BlockSpec((rows, width), lambda i: (i, 0))
    line = pl.BlockSpec((1, rows), lambda i: (0, i))
    return pl.pallas_call(
        small_kernel,
        grid=(total // rows,),
        in_specs=[half, half, block, line],
        out_specs=[block, line],
        out_shape=[
            jax.ShapeDtypeStruct((total, width), F32),
            jax.ShapeDtypeStruct((1, total), F32),
        ],
        compiler_params=pltpu.CompilerParams(vmem_limit_bytes=VMEM_LIMIT),
    )(left, right, weight, accum)


def after_kernel(*refs):
    del refs


def after(value, *others):
    place = pl.BlockSpec(memory_space=pl.ANY)
    return pl.pallas_call(
        after_kernel,
        grid=(1,),
        in_specs=[place] + [corner(other) for other in others],
        out_specs=place,
        out_shape=jax.ShapeDtypeStruct(value.shape, value.dtype),
        input_output_aliases={0: 0},
    )(value, *others)


def ring_sum(value, axis):
    size = lax.axis_size(axis)
    terms = [value]
    for step in range(1, size):
        terms.append(lax.ppermute(value, axis, [(i, (i + step) % size) for i in range(size)]))
    while len(terms) > 1:
        half = len(terms) // 2
        terms = [terms[i] + terms[i + half] for i in range(half)]
    return terms[0]


def body(
    pooled_grad,
    giant_slot,
    touched_rows,
    bag_lengths,
    small_ids,
    giant_weight,
    giant_accum,
    small_weight,
    small_accum,
):
    groups = lax.axis_size("row") * lax.axis_size("rep")
    owners = lax.axis_size("col")
    capacity = touched_rows.shape[3]
    width = small_weight.shape[2]
    samples = giant_slot.shape[2]
    exchange = functools.partial(lax.all_to_all, split_axis=0, concat_axis=0, tiled=True)

    pairs = pooled_grad[0].reshape(-1, owners, 2, width)
    small_values = exchange(pairs[:, :, 1, :].transpose(1, 0, 2), "col")
    lengths = bag_lengths[0, 0]
    small_counts = bag_counts(masked_ids(small_ids[0, 0], lengths[:, 1]), small_weight.shape[1])
    giant_counts = bag_counts(masked_ids(giant_slot[0, 0], lengths[:, 0]), groups * capacity)
    giant_out = after(pairs[:, :, 0, :].transpose(1, 0, 2), small_values, small_counts, giant_counts)
    giant_values = exchange(giant_out, "col").reshape(samples, width)

    left, right = bucket_sums(small_counts, small_values.reshape(samples, width))
    left = lax.psum_scatter(left, "rep", scatter_dimension=0, tiled=True)
    right = lax.psum_scatter(right, "rep", scatter_dimension=0, tiled=True)
    both = ring_sum(jnp.concatenate([left, right], axis=1), "row")
    left = lax.all_gather(both[:, : width // 2], "rep", axis=0, tiled=True)
    right = lax.all_gather(both[:, width // 2 :], "rep", axis=0, tiled=True)

    coded = packed_bucket_sums(giant_counts, giant_values, capacity, both)
    arrived = exchange(coded, ("row", "rep"))
    targets = touched_rows[0, :, 0, :].reshape(1, -1)
    new_gw, new_ga = giant_update(targets, arrived, giant_weight[0], giant_accum, capacity)
    new_sw, new_sa = small_update(left, right, small_weight[0], small_accum)
    return (new_gw[None], new_ga, new_sw[None], new_sa)


def solution(mesh):
    placed = (
        P(("row", "rep"), "col", None, None),
        P("col", ("row", "rep"), None, None),
        P("col", None, ("row", "rep"), None),
        P("col", ("row", "rep"), None, None),
        P("col", ("row", "rep"), None, None),
        P("col", ("row", "rep"), None),
        P("col", ("row", "rep")),
        P("col", None, None),
        P("col", None),
    )
    return jax.shard_map(
        body,
        mesh=mesh,
        in_specs=placed,
        out_specs=(
            P("col", ("row", "rep"), None),
            P("col", ("row", "rep")),
            P("col", None, None),
            P("col", None),
        ),
        check_vma=False,
    )
```

time: 405 us -> 299 us (0.74)
  the two profiles are of different devices: /device:TPU:64 before, /device:TPU:24 now
where the time goes in v1:
time: 299 us
  waiting for transfers between devices  102 us (34%)
  blocking collectives  67.2 us (22%)
  Pallas kernels  66.3 us (22%)
  starting transfers between devices  37.3 us (12%)
  between operations  14.2 us (5%)
  local copies, waits for them, and re-layouts  10.2 us (3%)
    pallas_call x2, Pallas kernels, bag_counts(): pl.pallas_call(counts_kernel, grid=(buckets // rows,), in_specs=[pl.Block...  47.5 us
    reduce_scatter x1, waiting for transfers between devices, body(): right = lax.psum_scatter(right, 'rep', scatter_dimension=0, tiled=True)  44.5 us
    reduce_scatter x1, waiting for transfers between devices, body(): left = lax.psum_scatter(left, 'rep', scatter_dimension=0, tiled=True)  42.4 us
    all_gather x1, blocking collectives, body(): left = lax.all_gather(both[:, :width // 2], 'rep', axis=0, tiled=True)  41.7 us
    all_gather x1, blocking collectives, body(): right = lax.all_gather(both[:, width // 2:], 'rep', axis=0, tiled=True)  25.6 us
    all_to_all x1, starting transfers between devices, body(): small_values = exchange(pairs[:, :, 1, :].transpose(1, 0, 2), 'col')  15.5 us
    ppermute x3, starting transfers between devices, ring_sum(): lax.ppermute(value, axis, [(i, (i + step) % size) for i in range(size)])  10.7 us
    all_to_all x1, waiting for transfers between devices, body(): small_values = exchange(pairs[:, :, 1, :].transpose(1, 0, 2), 'col')  10.1 us
  transfers between devices with their start and end apart: 8, of which 4 were waited for; matrix products, arithmetic and copies ran while one was open for 1% of the time, Pallas kernels for 18%

profile of v1, /device:TPU:24, one launch (start us, length us, event | category | flops | bytes accessed | tf_op | source)
XLA Modules:
  0.0 298.5 jit_solution(11885138318533285650)
XLA Ops:
  7.2 3.0 copy.14
  10.1 2.1 slice_bitcast_fusion
  12.2 0.0 copy-start.10
  12.2 0.0 copy-start.8
  12.2 15.5 %all-to-all-start = ((bf16[24,128,256]{2,1,0:T(8,128)(2,1)}), bf16[24,128,256]{2,1,0:T(8,128)(2,1)S(1)}, u32[]{:S(2)}, u32[]{:S(2)}) async-start(bf16[24,128,256]{2,1,0:T(8,128)(2,1)} %get-tuple-element.16), calls=%async_computation | async-start | bytes 3145728 | tf_op jit(solution)/shard_map/all_to_all | solution.py:262
  27.7 0.0 copy-done.10
  27.8 0.0 copy-done.8
  27.8 0.0 copy-start.9
  27.8 16.2 %shard_map.121.refs_2_.counts_ref = bf16[1024,3072]{1,0:T(8,128)(2,1)} custom-call(s32[8,3072]{1,0:T(8,128)S(1)} %fusion.ids_ref), custom_call_target="tpu_custom_call" | custom-call | flops 75497472 | bytes 6291456 | tf_op jit(solution)/shard_map/pallas_call | solution.py:47
  44.0 0.0 copy-done.9
  44.1 31.3 %shard_map.120.refs_3_.counts_ref = bf16[2048,3072]{1,0:T(8,128)(2,1)} custom-call(s32[8,3072]{1,0:T(8,128)S(1)} %fusion.1.ids_ref), custom_call_target="tpu_custom_call" | custom-call | flops 150994944 | bytes 12582912 | tf_op jit(solution)/shard_map/pallas_call | solution.py:47
  75.3 10.1 %all-to-all-done.refs_1_ = bf16[24,128,256]{2,1,0:T(8,128)(2,1)S(1)} async-done(((bf16[24,128,256]{2,1,0:T(8,128)(2,1)}), bf16[24,128,256]{2,1,0:T(8,128)(2,1)S(1)}, u32[]{:S(2)}, u32[]{:S(2)}) %all-to-all-start) | async-done | bytes 1572896 | tf_op jit(solution)/shard_map/all_to_all | solution.py:262
  85.4 0.0 copy-start
  85.4 1.2 copy-done
  86.6 0.7 shard_map.122
  87.3 0.0 copy-start.1
  87.3 4.4 %all-to-all-start.1 = ((bf16[24,128,256]{2,1,0:T(8,128)(2,1)}), bf16[24,128,256]{2,1,0:T(8,128)(2,1)S(1)}, u32[]{:S(2)}, u32[]{:S(2)}) async-start(bf16[24,128,256]{2,1,0:T(8,128)(2,1)} %shard_map.122), calls=%async_computation.1 | async-start | bytes 3145728 | tf_op jit(solution)/shard_map/all_to_all | solution.py:267
  91.7 0.0 reduce-scatter.3.cloned.1.call-start
  91.8 0.0 copy-done.1
  91.8 3.9 %shard_map.123 = (f32[1024,128]{1,0:T(8,128)S(1)}, f32[1024,128]{1,0:T(8,128)S(1)}) custom-call(bf16[1024,3072]{1,0:T(8,128)(2,1)} %shard_map.121.refs_2_.counts_ref, bf16[3072,256]{1,0:T(8,128)(2,1)S(1)} %bitcast.34), custom_call_target="tpu_custom_call" | custom-call | tf_op jit(solution)/shard_map/pallas_call | solution.py:97
  95.7 0.0 copy-start.3
  95.7 0.8 copy-done.3
  96.5 0.0 copy-start.4
  96.5 0.8 copy-done.4
  97.3 0.0 reduce-scatter.3.cloned.1.call-update
  97.3 0.0 reduce-scatter.5.cloned.1.call-start
  97.3 0.7 reduce-scatter.5.cloned.1.call-update
  98.0 42.4 %reduce-scatter.3.cloned.1.call-done = f32[128,128]{1,0:T(8,128)} async-done(((f32[1024,128]{1,0:T(8,128)}), f32[128,128]{1,0:T(8,128)}) %reduce-scatter.3.cloned.1.call-update) | async-done | bytes 65552 | tf_op jit(solution)/shard_map/reduce_scatter | solution.py:270
  140.5 0.8 constant_dynamic-update-slice_fusion.1
  141.3 44.5 %reduce-scatter.5.cloned.1.call-done = f32[128,128]{1,0:T(8,128)} async-done(((f32[1024,128]{1,0:T(8,128)}), f32[128,128]{1,0:T(8,128)}) %reduce-scatter.5.cloned.1.call-update) | async-done | bytes 65552 | tf_op jit(solution)/shard_map/reduce_scatter | solution.py:271
  185.9 0.8 constant_dynamic-update-slice_fusion
  186.7 3.3 %collective-permute-start.1 = (f32[128,256]{1,0:T(8,128)S(1)}, f32[128,256]{1,0:T(8,128)S(1)}, u32[]{:S(2)}, u32[]{:S(2)}) collective-permute-start(f32[128,256]{1,0:T(8,128)S(1)} %constant_dynamic-update-slice_fusion), channel_id=1, source_target_pairs={{0,8},{8,16},{16,24},{24,0},{1,9},{9,17},{17,25},{25,1},{2,10},{10... | collective-permute-start | bytes 393224 | tf_op jit(solution)/shard_map/ppermute | solution.py:236
  190.0 3.7 %collective-permute-start.2 = (f32[128,256]{1,0:T(8,128)S(1)}, f32[128,256]{1,0:T(8,128)S(1)}, u32[]{:S(2)}, u32[]{:S(2)}) collective-permute-start(f32[128,256]{1,0:T(8,128)S(1)} %constant_dynamic-update-slice_fusion), channel_id=1, source_target_pairs={{0,24},{8,0},{16,8},{24,16},{1,25},{9,1},{17,9},{25,17},{2,26},{10... | collective-permute-start | bytes 393224 | tf_op jit(solution)/shard_map/ppermute | solution.py:236
  193.8 3.7 %collective-permute-start = (f32[128,256]{1,0:T(8,128)S(1)}, f32[128,256]{1,0:T(8,128)S(1)}, u32[]{:S(2)}, u32[]{:S(2)}) collective-permute-start(f32[128,256]{1,0:T(8,128)S(1)} %constant_dynamic-update-slice_fusion), channel_id=1, source_target_pairs={{0,16},{8,24},{16,0},{24,8},{1,17},{9,25},{17,1},{25,9},{2,18},{10... | collective-permute-start | bytes 393224 | tf_op jit(solution)/shard_map/ppermute | solution.py:236
  197.4 0.0 collective-permute-done.1
  197.4 0.0 collective-permute-done.2
  197.4 4.7 %collective-permute-done = f32[128,256]{1,0:T(8,128)S(1)} collective-permute-done((f32[128,256]{1,0:T(8,128)S(1)}, f32[128,256]{1,0:T(8,128)S(1)}, u32[]{:S(2)}, u32[]{:S(2)}) %collective-permute-start) | collective-permute-done | bytes 131104 | tf_op jit(solution)/shard_map/ppermute | solution.py:236
  202.2 0.0 all-to-all-done.1
  202.2 8.4 %shard_map.124 = s16[32,144,128]{2,1,0:T(8,128)(2,1)} custom-call(bf16[2048,3072]{1,0:T(8,128)(2,1)} %shard_map.120.refs_3_.counts_ref, bf16[3072,256]{1,0:T(8,128)(2,1)S(1)} %bitcast.35, f32[128,256]{1,0:T(8,128)S(1)} %add_add_fusion.later_ref), custom_call_target="tpu_custom_call" | custom-call | tf_op jit(solution)/shard_map/pallas_call | solution.py:115
  210.5 0.0 copy-start.11
  210.5 0.0 copy-start.2
  210.5 0.0 copy-start.6
  210.5 6.6 %all-to-all-start.2 = ((s16[32,144,128]{2,1,0:T(8,128)(2,1)}), s16[32,144,128]{2,1,0:T(8,128)(2,1)S(1)}, u32[]{:S(2)}, u32[]{:S(2)}) async-start(s16[32,144,128]{2,1,0:T(8,128)(2,1)} %shard_map.124), calls=%async_computation.4 | async-start | bytes 2359296 | tf_op jit(solution)/shard_map/all_to_all | solution.py:277
  217.2 0.5 broadcast.3
  217.7 0.0 copy-done.11
  217.7 0.7 reduce.3
  218.4 0.1 reshape_squeeze.6.targets_ref
  218.5 0.0 copy-start.5
  218.5 0.0 copy-start.7
  218.5 41.7 %all_gather.6.left_ref = f32[1024,128]{1,0:T(8,128)S(1)} all-gather(f32[128,128]{1,0:T(8,128)S(1)} %get-tuple-element.19), channel_id=1, replica_groups=mesh['col'=24,'row'=4,'rep'=8] {'rep'}, dimensions={0}, use_global_device_ids=true | all-gather | bytes 589824 | tf_op jit(solution)/shard_map/all_gather | solution.py:273
  260.2 25.6 %all_gather.7.right_ref = f32[1024,128]{1,0:T(8,128)S(1)} all-gather(f32[128,128]{1,0:T(8,128)S(1)} %get-tuple-element.18), channel_id=1, replica_groups=mesh['col'=24,'row'=4,'rep'=8] {'rep'}, dimensions={0}, use_global_device_ids=true | all-gather | bytes 589824 | tf_op jit(solution)/shard_map/all_gather | solution.py:274
  285.7 0.0 copy-done.2
  285.7 0.0 copy-done.6
  285.7 1.7 shard_map.126
  287.4 0.0 all-to-all-done.2.arrived_ref
  287.4 0.0 copy-done.5
  287.5 0.0 copy-done.7
  287.5 4.2 %shard_map.125 = (f32[512,256]{1,0:T(8,128)}, f32[1,512]{1,0:T(1,128)}) custom-call(s32[1,2048]{1,0:T(1,128)S(1)} %reshape_squeeze.6.targets_ref, s16[32,144,128]{2,1,0:T(8,128)(2,1)S(1)} %all-to-all-done.2.arrived_ref, f32[512,256]{1,0:T(8,128)S(1)} %bitcast.37, f32[1,512]{1,0:T(1,128)S(1)} %copy-done.7), custom_call_target="tpu_custom_call" | custom-call | tf_op jit(solution)/shard_map/pallas_call | solution.py:170
  (5 shorter events, 0.1 us)
Async XLA Ops:
  12.2 15.5 %copy-start.10 = (s32[1,1,3072,2]{2,3,1,0:T(2,128)S(1)}, s32[1,1,3072,2]{2,3,1,0:T(2,128)}, u32[]{:S(2)}) copy-start(s32[1,1,3072,2]{2,3,1,0:T(2,128)} %param.12) | copy-start | bytes 73732
  12.2 15.6 %copy-start.8 = (s32[1,1,3072,8]{2,3,1,0:T(8,128)S(1)}, s32[1,1,3072,8]{2,3,1,0:T(8,128)}, u32[]{:S(2)}) copy-start(s32[1,1,3072,8]{2,3,1,0:T(8,128)} %param.13) | copy-start | bytes 294916
  12.2 73.2 %all-to-all-start = ((bf16[24,128,256]{2,1,0:T(8,128)(2,1)}), bf16[24,128,256]{2,1,0:T(8,128)(2,1)S(1)}, u32[]{:S(2)}, u32[]{:S(2)}) async-start(bf16[24,128,256]{2,1,0:T(8,128)(2,1)} %get-tuple-element.16), calls=%async_computation | async-start | bytes 3145728 | tf_op jit(solution)/shard_map/all_to_all | solution.py:262
  27.8 16.2 %copy-start.9 = (s32[1,1,3072,8]{2,3,1,0:T(8,128)S(1)}, s32[1,1,3072,8]{2,3,1,0:T(8,128)}, u32[]{:S(2)}) copy-start(s32[1,1,3072,8]{2,3,1,0:T(8,128)} %param.10) | copy-start | bytes 294916
  85.4 1.2 copy-start
  87.3 4.4 %copy-start.1 = (bf16[24,128,256]{2,1,0:T(8,128)(2,1)S(1)}, bf16[24,128,256]{2,1,0:T(8,128)(2,1)}, u32[]{:S(2)}) copy-start(bf16[24,128,256]{2,1,0:T(8,128)(2,1)} %copy-done) | copy-start | bytes 4718596
  87.3 114.8 %all-to-all-start.1 = ((bf16[24,128,256]{2,1,0:T(8,128)(2,1)}), bf16[24,128,256]{2,1,0:T(8,128)(2,1)S(1)}, u32[]{:S(2)}, u32[]{:S(2)}) async-start(bf16[24,128,256]{2,1,0:T(8,128)(2,1)} %shard_map.122), calls=%async_computation.1 | async-start | bytes 3145728 | tf_op jit(solution)/shard_map/all_to_all | solution.py:267
  91.7 48.7 %reduce-scatter.3.cloned.1.call-start = ((), (), s32[]{:S(2)}) async-start(), calls=%async_computation.5 | async-start | bytes 589824 | tf_op jit(solution)/shard_map/reduce_scatter | solution.py:270
  95.7 0.8 copy-start.3
  96.5 0.8 copy-start.4
  97.3 88.6 %reduce-scatter.5.cloned.1.call-start = ((), (), s32[]{:S(2)}) async-start(), calls=%async_computation.6 | async-start | bytes 589824 | tf_op jit(solution)/shard_map/reduce_scatter | solution.py:271
  186.7 10.7 %collective-permute-start.1 = (f32[128,256]{1,0:T(8,128)S(1)}, f32[128,256]{1,0:T(8,128)S(1)}, u32[]{:S(2)}, u32[]{:S(2)}) collective-permute-start(f32[128,256]{1,0:T(8,128)S(1)} %constant_dynamic-update-slice_fusion), channel_id=1, source_target_pairs={{0,8},{8,16},{16,24},{24,0},{1,9},{9,17},{17,25},{25,1},{2,10},{10... | collective-permute-start | bytes 393224 | tf_op jit(solution)/shard_map/ppermute | solution.py:236
  190.0 7.4 %collective-permute-start.2 = (f32[128,256]{1,0:T(8,128)S(1)}, f32[128,256]{1,0:T(8,128)S(1)}, u32[]{:S(2)}, u32[]{:S(2)}) collective-permute-start(f32[128,256]{1,0:T(8,128)S(1)} %constant_dynamic-update-slice_fusion), channel_id=1, source_target_pairs={{0,24},{8,0},{16,8},{24,16},{1,25},{9,1},{17,9},{25,17},{2,26},{10... | collective-permute-start | bytes 393224 | tf_op jit(solution)/shard_map/ppermute | solution.py:236
  193.8 8.4 %collective-permute-start = (f32[128,256]{1,0:T(8,128)S(1)}, f32[128,256]{1,0:T(8,128)S(1)}, u32[]{:S(2)}, u32[]{:S(2)}) collective-permute-start(f32[128,256]{1,0:T(8,128)S(1)} %constant_dynamic-update-slice_fusion), channel_id=1, source_target_pairs={{0,16},{8,24},{16,0},{24,8},{1,17},{9,25},{17,1},{25,9},{2,18},{10... | collective-permute-start | bytes 393224 | tf_op jit(solution)/shard_map/ppermute | solution.py:236
  210.5 7.2 %copy-start.11 = (s32[1,32,1,64]{3,2,1,0:T(1,128)S(1)}, s32[1,32,1,64]{3,2,1,0:T(1,128)}, u32[]{:S(2)}) copy-start(s32[1,32,1,64]{3,2,1,0:T(1,128)} %param.11) | copy-start | bytes 24580
  210.5 75.2 %copy-start.2 = (f32[1,1024,256]{2,1,0:T(8,128)S(1)}, f32[1,1024,256]{2,1,0:T(8,128)}, u32[]{:S(2)}) copy-start(f32[1,1024,256]{2,1,0:T(8,128)} %param.16) | copy-start | bytes 3145732
  210.5 75.2 %copy-start.6 = (f32[1,1024]{1,0:T(1,128)S(1)}, f32[1,1024]{1,0:T(1,128)}, u32[]{:S(2)}) copy-start(f32[1,1024]{1,0:T(1,128)} %accum_ref.3) | copy-start | bytes 12292
  210.5 76.9 %all-to-all-start.2 = ((s16[32,144,128]{2,1,0:T(8,128)(2,1)}), s16[32,144,128]{2,1,0:T(8,128)(2,1)S(1)}, u32[]{:S(2)}, u32[]{:S(2)}) async-start(s16[32,144,128]{2,1,0:T(8,128)(2,1)} %shard_map.124), calls=%async_computation.4 | async-start | bytes 2359296 | tf_op jit(solution)/shard_map/all_to_all | solution.py:277
  218.5 69.0 %copy-start.5 = (f32[1,512,256]{2,1,0:T(8,128)S(1)}, f32[1,512,256]{2,1,0:T(8,128)}, u32[]{:S(2)}) copy-start(f32[1,512,256]{2,1,0:T(8,128)} %param.14) | copy-start | bytes 1572868
  218.5 69.0 %copy-start.7 = (f32[1,512]{1,0:T(1,128)S(1)}, f32[1,512]{1,0:T(1,128)}, u32[]{:S(2)}) copy-start(f32[1,512]{1,0:T(1,128)} %accum_ref.2) | copy-start | bytes 6148
Sparse Core Ops, SparseCore 0:
  97.4 43.0 reduce-scatter.2
  144.4 41.3 reduce-scatter.4

commit v2 on v1

v2 whole, which is shorter than its diff:
```python
import functools

import jax
import jax.numpy as jnp
from jax import lax
from jax.experimental import pallas as pl
from jax.experimental.pallas import tpu as pltpu
from jax.sharding import PartitionSpec as P

LEARN = 0.5
TINY = 1e-08
BF = jnp.bfloat16
F32 = jnp.float32
VMEM_LIMIT = 20 * 1024 * 1024
TAG_ROWS = 16


def masked_ids(ids, lengths):
    live = lax.broadcasted_iota(jnp.int32, ids.shape, 1) < lengths[:, None]
    return jnp.where(live, ids, -1).T


def counts_kernel(ids_ref, out_ref):
    rows, samples = out_ref.shape
    bag = ids_ref.shape[0]
    lanes = 256
    first = pl.program_id(0) * rows
    local = lax.broadcasted_iota(jnp.int32, (16, lanes), 0)

    @pl.loop(0, samples // lanes)
    def _(chunk):
        at = pl.ds(pl.multiple_of(chunk * lanes, lanes), lanes)
        named = [jnp.broadcast_to(ids_ref[k : k + 1, at], (16, lanes)) for k in range(bag)]

        @pl.loop(0, rows // 16)
        def _(step):
            bucket = local + (first + step * 16)
            total = jnp.zeros((16, lanes), F32)
            for k in range(bag):
                total = total + jnp.where(named[k] == bucket, 1.0, 0.0)
            out_ref[pl.ds(pl.multiple_of(step * 16, 16), 16), at] = total.astype(BF)


def bag_counts(ids, buckets):
    bag, samples = ids.shape
    rows = 256
    return pl.pallas_call(
        counts_kernel,
        grid=(buckets // rows,),
        in_specs=[pl.BlockSpec((bag, samples), lambda i: (0, 0))],
        out_specs=pl.BlockSpec((rows, samples), lambda i: (i, 0)),
        out_shape=jax.ShapeDtypeStruct((buckets, samples), BF),
        compiler_params=pltpu.CompilerParams(vmem_limit_bytes=VMEM_LIMIT),
        cost_estimate=pl.CostEstimate(
            flops=3 * bag * buckets * samples, bytes_accessed=2 * buckets * samples, transcendentals=0
        ),
    )(ids)


def corner(array):
    lead = (1,) * (array.ndim - 2)
    return pl.BlockSpec(lead + (16, 128), lambda *_: (0,) * array.ndim)


def matmul_kernel(counts_ref, values_ref, out_ref):
    out_ref[...] = jnp.dot(counts_ref[...], values_ref[...], preferred_element_type=F32)


def coded_rows(sums):
    largest = jnp.maximum(jnp.max(jnp.abs(sums), axis=1, keepdims=True), 2.0**-100)
    power = jnp.floor(jnp.log2(largest) + 1e-3) - 14.0
    coded = jnp.clip(jnp.round(sums * jnp.exp2(-power)), -32767.0, 32767.0)
    return coded.astype(jnp.int32).astype(jnp.int16), power


def packed_kernel(capacity, place_ref, counts_ref, values_ref, *refs):
    terms, out_ref = refs[:-1], refs[-1]
    sums = jnp.dot(counts_ref[...], values_ref[...], preferred_element_type=F32)
    coded, power = coded_rows(sums)
    rows, width = sums.shape
    lanes = out_ref.shape[2]
    mine = terms[0].shape[0] // len(terms)
    at = pl.ds(pl.multiple_of(place_ref[0] * mine, mine), mine)
    small = terms[0][at, :]
    for term in terms[1:]:
        small = small + term[at, :]
    small_coded, small_power = coded_rows(small)
    tall = capacity + mine
    diagonal = lax.broadcasted_iota(jnp.int32, (tall, lanes), 0) == lax.broadcasted_iota(jnp.int32, (tall, lanes), 1)
    for block in range(rows // capacity):
        slots = slice(block * capacity, (block + 1) * capacity)
        first = 0
        for piece, count in ((coded[slots, :], capacity), (small_coded, mine)):
            for part in range(width // lanes):
                out_ref[block, first : first + count, :] = piece[:, part * lanes : (part + 1) * lanes]
                first += count
        powers = jnp.concatenate([power[slots, :], small_power], axis=0)
        spread = jnp.where(diagonal, jnp.broadcast_to(powers, (tall, lanes)), 0.0)
        tag = jnp.broadcast_to(jnp.sum(spread, axis=0, keepdims=True), (TAG_ROWS, lanes))
        out_ref[block, first:, :] = tag.astype(jnp.int32).astype(jnp.int16)


def bucket_sums(counts, values):
    buckets, samples = counts.shape
    width = values.shape[1]
    rows = 512
    return pl.pallas_call(
        matmul_kernel,
        grid=(buckets // rows,),
        in_specs=[
            pl.BlockSpec((rows, samples), lambda i: (i, 0)),
            pl.BlockSpec((samples, width), lambda i: (0, 0)),
        ],
        out_specs=pl.BlockSpec((rows, width), lambda i: (i, 0)),
        out_shape=jax.ShapeDtypeStruct((buckets, width), F32),
        compiler_params=pltpu.CompilerParams(vmem_limit_bytes=VMEM_LIMIT),
    )(counts, values)


def packed_bucket_sums(counts, values, capacity, place, terms):
    buckets, samples = counts.shape
    width = values.shape[1]
    rows, lanes = 512, 128
    mine = terms[0].shape[0] // len(terms)
    tall = (capacity + mine) * width // lanes + TAG_ROWS
    whole = pl.BlockSpec(terms[0].shape, lambda i: (0, 0))
    return pl.pallas_call(
        functools.partial(packed_kernel, capacity),
        grid=(buckets // rows,),
        in_specs=[
            pl.BlockSpec(memory_space=pltpu.SMEM),
            pl.BlockSpec((rows, samples), lambda i: (i, 0)),
            pl.BlockSpec((samples, width), lambda i: (0, 0)),
        ]
        + [whole] * len(terms),
        out_specs=pl.BlockSpec((rows // capacity, tall, lanes), lambda i: (i, 0, 0)),
        out_shape=jax.ShapeDtypeStruct((buckets // capacity, tall, lanes), jnp.int16),
        compiler_params=pltpu.CompilerParams(vmem_limit_bytes=VMEM_LIMIT),
    )(place, counts, values, *terms)


def adagrad_step(weight, accum, grad):
    rows, width = grad.shape
    column = jnp.broadcast_to(accum, (8, rows)).T[:, 0:1]
    total = column + jnp.sum(grad * grad, axis=1, keepdims=True) * (1.0 / width)
    new_weight = weight - grad * (LEARN / (jnp.sqrt(total) + TINY))
    return new_weight, jnp.broadcast_to(total, (rows, 128)).T[0:1, :]


def decoded(coded, scale):
    return coded.astype(jnp.int32).astype(F32) * scale


def update_kernel(
    capacity,
    outer,
    targets_ref,
    arrived_ref,
    giant_weight_ref,
    giant_accum_ref,
    small_weight_ref,
    small_accum_ref,
    new_giant_weight_ref,
    new_giant_accum_ref,
    new_small_weight_ref,
    new_small_accum_ref,
    parts,
):
    rows, width = giant_weight_ref.shape
    groups, tall, lanes = arrived_ref.shape
    halves = width // lanes
    mine = (tall - TAG_ROWS) // halves - capacity

    def scales(group):
        tag = arrived_ref[group, tall - TAG_ROWS :, :].astype(jnp.int32).astype(F32)
        return jnp.exp2(tag.T[:, 0:1])

    @pl.when(pl.program_id(0) == 0)
    def _():
        for group in range(groups):
            here = slice(group * capacity, (group + 1) * capacity)
            scale = scales(group)[0:capacity]
            for part in range(halves):
                value = decoded(arrived_ref[group, part * capacity : (part + 1) * capacity, :], scale)
                high = value.astype(BF)
                rest = value - high.astype(F32)
                middle = rest.astype(BF)
                low = (rest - middle.astype(F32)).astype(BF)
                for place, piece in enumerate((high, middle, low)):
                    at = place * width + part * lanes
                    parts[here, at : at + lanes] = piece

    sources = groups * capacity
    row = lax.broadcasted_iota(jnp.int32, (rows, sources), 0) + pl.program_id(0) * rows
    hit = jnp.where(jnp.broadcast_to(targets_ref[...], (rows, sources)) == row, 1.0, 0.0).astype(BF)
    product = jnp.dot(hit, parts[...], preferred_element_type=F32)
    grad = product[:, 0:width] + (product[:, width : 2 * width] + product[:, 2 * width :])
    new_weight, new_accum = adagrad_step(giant_weight_ref[...], giant_accum_ref[...], grad)
    new_giant_weight_ref[...] = new_weight
    new_giant_accum_ref[...] = new_accum

    band = outer * mine
    inner = groups // outer
    bands = small_weight_ref.shape[0] // band
    for local in range(bands):
        at = slice(local * band, (local + 1) * band)
        pieces = []
        for place in range(outer):
            group = place * inner + pl.program_id(0) * bands + local
            scale = scales(group)[capacity : capacity + mine]
            pair = []
            for part in range(halves):
                first = halves * capacity + part * mine
                pair.append(decoded(arrived_ref[group, first : first + mine, :], scale))
            pieces.append(jnp.concatenate(pair, axis=1))
        grad = jnp.concatenate(pieces, axis=0)
        new_weight, new_accum = adagrad_step(small_weight_ref[at, :], small_accum_ref[:, at], grad)
        new_small_weight_ref[at, :] = new_weight
        new_small_accum_ref[:, at] = new_accum


def update(targets, arrived, giant_weight, giant_accum, small_weight, small_accum, capacity, outer):
    giant_rows, width = giant_weight.shape
    small_rows = small_weight.shape[0]
    sources = targets.shape[1]
    steps = 4

    def blocks(rows):
        return [pl.BlockSpec((rows // steps, width), lambda i: (i, 0)), pl.BlockSpec((1, rows // steps), lambda i: (0, i))]

    def shapes(rows):
        return [jax.ShapeDtypeStruct((rows, width), F32), jax.ShapeDtypeStruct((1, rows), F32)]

    return pl.pallas_call(
        functools.partial(update_kernel, capacity, outer),
        grid=(steps,),
        in_specs=[
            pl.BlockSpec((1, sources), lambda i: (0, 0)),
            pl.BlockSpec(arrived.shape, lambda i: (0, 0, 0)),
        ]
        + blocks(giant_rows)
        + blocks(small_rows),
        out_specs=blocks(giant_rows) + blocks(small_rows),
        out_shape=shapes(giant_rows) + shapes(small_rows),
        scratch_shapes=[pltpu.VMEM((sources, 3 * width), BF)],
        compiler_params=pltpu.CompilerParams(vmem_limit_bytes=VMEM_LIMIT),
    )(targets, arrived, giant_weight, giant_accum, small_weight, small_accum)


def after_kernel(*refs):
    del refs


def after(value, *others):
    place = pl.BlockSpec(memory_space=pl.ANY)
    return pl.pallas_call(
        after_kernel,
        grid=(1,),
        in_specs=[place] + [corner(other) for other in others],
        out_specs=place,
        out_shape=jax.ShapeDtypeStruct(value.shape, value.dtype),
        input_output_aliases={0: 0},
    )(value, *others)


def ring_terms(value, axis):
    size = lax.axis_size(axis)
    terms = [value]
    for step in range(1, size):
        terms.append(lax.ppermute(value, axis, [(i, (i + step) % size) for i in range(size)]))
    return terms


def body(
    pooled_grad,
    giant_slot,
    touched_rows,
    bag_lengths,
    small_ids,
    giant_weight,
    giant_accum,
    small_weight,
    small_accum,
):
    groups = lax.axis_size("row") * lax.axis_size("rep")
    owners = lax.axis_size("col")
    capacity = touched_rows.shape[3]
    width = small_weight.shape[2]
    samples = giant_slot.shape[2]
    exchange = functools.partial(lax.all_to_all, split_axis=0, concat_axis=0, tiled=True)

    pairs = pooled_grad[0].reshape(-1, owners, 2, width)
    small_values = exchange(pairs[:, :, 1, :].transpose(1, 0, 2), "col")
    lengths = bag_lengths[0, 0]
    small_counts = bag_counts(masked_ids(small_ids[0, 0], lengths[:, 1]), small_weight.shape[1])
    giant_counts = bag_counts(masked_ids(giant_slot[0, 0], lengths[:, 0]), groups * capacity)
    small_sum = bucket_sums(small_counts, small_values.reshape(samples, width))

    giant_out = after(pairs[:, :, 0, :].transpose(1, 0, 2), small_sum, giant_counts)
    giant_values = exchange(giant_out, "col").reshape(samples, width)

    small_sum = lax.psum_scatter(small_sum, "rep", scatter_dimension=0, tiled=True)
    terms = ring_terms(small_sum, "row")
    place = lax.axis_index("row").astype(jnp.int32).reshape(1)

    packed = packed_bucket_sums(giant_counts, giant_values, capacity, place, terms)
    arrived = exchange(packed, ("row", "rep"))
    targets = touched_rows[0, :, 0, :].reshape(1, -1)
    new_gw, new_ga, new_sw, new_sa = update(
        targets, arrived, giant_weight[0], giant_accum, small_weight[0], small_accum, capacity, len(terms)
    )
    return (new_gw[None], new_ga, new_sw[None], new_sa)


def solution(mesh):
    placed = (
        P(("row", "rep"), "col", None, None),
        P("col", ("row", "rep"), None, None),
        P("col", None, ("row", "rep"), None),
        P("col", ("row", "rep"), None, None),
        P("col", ("row", "rep"), None, None),
        P("col", ("row", "rep"), None),
        P("col", ("row", "rep")),
        P("col", None, None),
        P("col", None),
    )
    return jax.shard_map(
        body,
        mesh=mesh,
        in_specs=placed,
        out_specs=(
            P("col", ("row", "rep"), None),
            P("col", ("row", "rep")),
            P("col", None, None),
            P("col", None),
        ),
        check_vma=False,
    )
```

time: 299 us -> 231 us (0.77)
  the two profiles are of different devices: /device:TPU:24 before, /device:TPU:8 now
where the time goes in v2:
time: 231 us; the launch traced here: 230 us
  waiting for transfers between devices  94.2 us (41%)
  Pallas kernels  61.3 us (27%)
  starting transfers between devices  39 us (17%)
  local copies, waits for them, and re-layouts  21 us (9%)
  between operations  14.2 us (6%)
    reduce_scatter x1, waiting for transfers between devices, body(): lax.psum_scatter(small_sum, 'rep', scatter_dimension=0, tiled=True)  48.1 us
    pallas_call x2, Pallas kernels, bag_counts(): pl.pallas_call(counts_kernel, grid=(buckets // rows,), in_specs=[pl.Block...  45.1 us
    all_to_all x1, waiting for transfers between devices, body(): arrived = exchange(packed, ('row', 'rep'))  36.4 us
    unnamed x28, local copies, waits for them, and re-layouts  18.9 us
    all_to_all x1, starting transfers between devices, body(): small_values = exchange(pairs[:, :, 1, :].transpose(1, 0, 2), 'col')  15.5 us
    ppermute x3, starting transfers between devices, ring_terms(): lax.ppermute(value, axis, [(i, (i + step) % size) for i in range(size)])  11.3 us
    all_to_all x1, starting transfers between devices, body(): arrived = exchange(packed, ('row', 'rep'))  7.91 us
    pallas_call x1, Pallas kernels, packed_bucket_sums(): pl.pallas_call(functools.partial(packed_kernel, capacity), grid=(buckets...  6.59 us
  transfers between devices with their start and end apart: 7, of which 5 were waited for; matrix products, arithmetic and copies ran while one was open for 1% of the time, Pallas kernels for 20%

profile of v2, /device:TPU:8, one launch (start us, length us, event | category | flops | bytes accessed | tf_op | source)
XLA Modules:
  0.0 230.4 jit_solution(727642590211892613)
XLA Ops:
  7.2 3.0 %copy.14 = bf16[1,128,48,256]{3,1,2,0:T(8,128)(2,1)S(1)} copy(bf16[1,128,48,256]{3,2,1,0:T(8,128)(2,1)} %param.9) | data formatting | bytes 6291456 | tf_op args[0]
  10.1 2.0 slice_bitcast_fusion
  12.2 0.0 copy-start.11
  12.2 0.0 copy-start.9
  12.2 15.5 %all-to-all-start = ((bf16[24,128,256]{2,1,0:T(8,128)(2,1)}), bf16[24,128,256]{2,1,0:T(8,128)(2,1)S(1)}, u32[]{:S(2)}, u32[]{:S(2)}) async-start(bf16[24,128,256]{2,1,0:T(8,128)(2,1)} %get-tuple-element.12), calls=%async_computation | async-start | bytes 3145728 | tf_op jit(solution)/shard_map/all_to_all | solution.py:293
  27.7 0.0 copy-done.11
  27.7 0.0 copy-done.9
  27.7 0.0 copy-start.10
  27.8 15.0 %shard_map.121.counts_ref = bf16[1024,3072]{1,0:T(8,128)(2,1)S(1)} custom-call(s32[8,3072]{1,0:T(8,128)S(1)} %fusion.ids_ref), custom_call_target="tpu_custom_call" | custom-call | flops 75497472 | bytes 6291456 | tf_op jit(solution)/shard_map/pallas_call | solution.py:47
  42.8 0.0 copy-start.2
  42.8 2.6 %copy-done.2 = bf16[1024,3072]{1,0:T(8,128)(2,1)} copy-done((bf16[1024,3072]{1,0:T(8,128)(2,1)}, bf16[1024,3072]{1,0:T(8,128)(2,1)S(1)}, u32[]{:S(2)}) %copy-start.2) | copy-done | bytes 6291480
  45.4 0.0 copy-done.10
  45.4 30.1 %shard_map.120.refs_2_.counts_ref = bf16[2048,3072]{1,0:T(8,128)(2,1)S(1)} custom-call(s32[8,3072]{1,0:T(8,128)S(1)} %fusion.1.ids_ref), custom_call_target="tpu_custom_call" | custom-call | flops 150994944 | bytes 12582912 | tf_op jit(solution)/shard_map/pallas_call | solution.py:47
  75.5 0.0 copy-start
  75.5 4.5 %copy-done = bf16[2048,3072]{1,0:T(8,128)(2,1)} copy-done((bf16[2048,3072]{1,0:T(8,128)(2,1)}, bf16[2048,3072]{1,0:T(8,128)(2,1)S(1)}, u32[]{:S(2)}) %copy-start) | copy-done | bytes 12582936
  80.0 5.4 %all-to-all-done = bf16[24,128,256]{2,1,0:T(8,128)(2,1)S(1)} async-done(((bf16[24,128,256]{2,1,0:T(8,128)(2,1)}), bf16[24,128,256]{2,1,0:T(8,128)(2,1)S(1)}, u32[]{:S(2)}, u32[]{:S(2)}) %all-to-all-start) | async-done | bytes 1572896 | tf_op jit(solution)/shard_map/all_to_all | solution.py:293
  85.4 0.0 copy-start.3
  85.4 2.8 %copy-done.3 = bf16[1024,3072]{1,0:T(8,128)(2,1)S(1)} copy-done((bf16[1024,3072]{1,0:T(8,128)(2,1)S(1)}, bf16[1024,3072]{1,0:T(8,128)(2,1)}, u32[]{:S(2)}) %copy-start.3) | copy-done | bytes 6291480
  88.2 2.8 %shard_map.122.refs_1_ = f32[1024,256]{1,0:T(8,128)} custom-call(bf16[1024,3072]{1,0:T(8,128)(2,1)S(1)} %copy-done.3, bf16[3072,256]{1,0:T(8,128)(2,1)S(1)} %bitcast.34), custom_call_target="tpu_custom_call" | custom-call | tf_op jit(solution)/shard_map/pallas_call | solution.py:107
  90.9 0.7 shard_map.123
  91.6 4.3 %all-to-all-start.1 = ((bf16[24,128,256]{2,1,0:T(8,128)(2,1)}), bf16[24,128,256]{2,1,0:T(8,128)(2,1)S(1)}, u32[]{:S(2)}, u32[]{:S(2)}) async-start(bf16[24,128,256]{2,1,0:T(8,128)(2,1)} %shard_map.123), calls=%async_computation.1 | async-start | bytes 3145728 | tf_op jit(solution)/shard_map/all_to_all | solution.py:300
  96.0 0.0 reduce-scatter.2.cloned.1.call-start
  96.0 0.7 reduce-scatter.2.cloned.1.call-update
  96.7 48.1 %reduce-scatter.2.cloned.1.call-done.refs_0_ = f32[128,256]{1,0:T(8,128)} async-done(((f32[1024,256]{1,0:T(8,128)}), f32[128,256]{1,0:T(8,128)}) %reduce-scatter.2.cloned.1.call-update) | async-done | bytes 131088 | tf_op jit(solution)/shard_map/reduce_scatter | solution.py:302
  144.9 3.3 %collective-permute-start = (f32[128,256]{1,0:T(8,128)}, f32[128,256]{1,0:T(8,128)S(1)}, u32[]{:S(2)}, u32[]{:S(2)}) collective-permute-start(f32[128,256]{1,0:T(8,128)} %reduce-scatter.2.cloned.1.call-done.refs_0_), channel_id=1, source_target_pairs={{0,8},{8,16},{16,24},{24,0},{1,9},{9,17},{17,25},{25,1},{2,10},{10... | collective-permute-start | bytes 393224 | tf_op jit(solution)/shard_map/ppermute | solution.py:270
  148.1 4.6 %collective-permute-start.1 = (f32[128,256]{1,0:T(8,128)}, f32[128,256]{1,0:T(8,128)S(1)}, u32[]{:S(2)}, u32[]{:S(2)}) collective-permute-start(f32[128,256]{1,0:T(8,128)} %reduce-scatter.2.cloned.1.call-done.refs_0_), channel_id=1, source_target_pairs={{0,16},{8,24},{16,0},{24,8},{1,17},{9,25},{17,1},{25,9},{2,18},{10... | collective-permute-start | bytes 393224 | tf_op jit(solution)/shard_map/ppermute | solution.py:270
  152.7 3.4 %collective-permute-start.2 = (f32[128,256]{1,0:T(8,128)}, f32[128,256]{1,0:T(8,128)S(1)}, u32[]{:S(2)}, u32[]{:S(2)}) collective-permute-start(f32[128,256]{1,0:T(8,128)} %reduce-scatter.2.cloned.1.call-done.refs_0_), channel_id=1, source_target_pairs={{0,24},{8,0},{16,8},{24,16},{1,25},{9,1},{17,9},{25,17},{2,26},{10... | collective-permute-start | bytes 393224 | tf_op jit(solution)/shard_map/ppermute | solution.py:270
  156.1 0.0 collective-permute-done.refs_1_
  156.2 0.6 collective-permute-done.1.refs_2_
  156.7 3.1 %collective-permute-done.2.refs_3_ = f32[128,256]{1,0:T(8,128)S(1)} collective-permute-done((f32[128,256]{1,0:T(8,128)}, f32[128,256]{1,0:T(8,128)S(1)}, u32[]{:S(2)}, u32[]{:S(2)}) %collective-permute-start.2) | collective-permute-done | bytes 131104 | tf_op jit(solution)/shard_map/ppermute | solution.py:270
  159.8 0.0 all-to-all-done.1
  159.8 0.0 copy-start.1
  159.8 4.6 %copy-done.1 = bf16[2048,3072]{1,0:T(8,128)(2,1)S(1)} copy-done((bf16[2048,3072]{1,0:T(8,128)(2,1)S(1)}, bf16[2048,3072]{1,0:T(8,128)(2,1)}, u32[]{:S(2)}) %copy-start.1) | copy-done | bytes 12582936
  164.4 0.0 copy-start.6
  164.4 0.9 copy-done.6
  165.3 6.6 %shard_map.124 = s16[32,208,128]{2,1,0:T(8,128)(2,1)} custom-call(s32[1]{0:T(128)} %bitcast.place_ref, bf16[2048,3072]{1,0:T(8,128)(2,1)S(1)} %copy-done.1, bf16[3072,256]{1,0:T(8,128)(2,1)S(1)} %bitcast.33, f32[128,256]{1,0:T(8,128)S(1)} %copy-done.6, f32[128,256]{1,0:T(8,128)S(1)} %collective-permute-done.refs_1_, ...), custom_call_target="tpu_custom_call" | custom-call | tf_op jit(solution)/shard_map/pallas_call | solution.py:127
  171.9 0.0 copy-start.12
  171.9 0.0 copy-start.4
  171.9 0.0 copy-start.5
  171.9 0.0 copy-start.7
  171.9 0.0 copy-start.8
  171.9 7.9 %all-to-all-start.2 = ((s16[32,208,128]{2,1,0:T(8,128)(2,1)}), s16[32,208,128]{2,1,0:T(8,128)(2,1)S(1)}, u32[]{:S(2)}, u32[]{:S(2)}) async-start(s16[32,208,128]{2,1,0:T(8,128)(2,1)} %shard_map.124), calls=%async_computation.3 | async-start | bytes 3407872 | tf_op jit(solution)/shard_map/all_to_all | solution.py:307
  179.8 0.5 broadcast.3
  180.3 0.0 copy-done.12
  180.3 0.7 reduce.3
  181.0 0.1 reshape_squeeze.6.targets_ref
  181.1 36.4 %all-to-all-done.2.arrived_ref = s16[32,208,128]{2,1,0:T(8,128)(2,1)S(1)} async-done(((s16[32,208,128]{2,1,0:T(8,128)(2,1)}), s16[32,208,128]{2,1,0:T(8,128)(2,1)S(1)}, u32[]{:S(2)}, u32[]{:S(2)}) %all-to-all-start.2) | async-done | bytes 1703968 | tf_op jit(solution)/shard_map/all_to_all | solution.py:307
  217.5 0.0 copy-done.4
  217.5 0.0 copy-done.5
  217.5 0.0 copy-done.7
  217.5 0.0 copy-done.8
  217.5 6.1 %shard_map.125 = (f32[512,256]{1,0:T(8,128)}, f32[1,512]{1,0:T(1,128)}, f32[1024,256]{1,0:T(8,128)}, f32[1,1024]{1,0:T(1,128)}) custom-call(s32[1,2048]{1,0:T(1,128)S(1)} %reshape_squeeze.6.targets_ref, s16[32,208,128]{2,1,0:T(8,128)(2,1)S(1)} %all-to-all-done.2.arrived_ref, f32[512,256]{1,0:T(8,128)S(1)} %bitcast.36, f32[1,512]{1,0:T(1,128)S(1)} %copy-done.8, ...), custom_call_target="tpu_custom_call" | custom-call | tf_op jit(solution)/shard_map/pallas_call | solution.py:234
  (3 shorter events, 0.1 us)
Async XLA Ops:
  12.2 15.5 %copy-start.11 = (s32[1,1,3072,2]{2,3,1,0:T(2,128)S(1)}, s32[1,1,3072,2]{2,3,1,0:T(2,128)}, u32[]{:S(2)}) copy-start(s32[1,1,3072,2]{2,3,1,0:T(2,128)} %param.12) | copy-start | bytes 73732
  12.2 15.6 %copy-start.9 = (s32[1,1,3072,8]{2,3,1,0:T(8,128)S(1)}, s32[1,1,3072,8]{2,3,1,0:T(8,128)}, u32[]{:S(2)}) copy-start(s32[1,1,3072,8]{2,3,1,0:T(8,128)} %param.13) | copy-start | bytes 294916
  12.2 73.2 %all-to-all-start = ((bf16[24,128,256]{2,1,0:T(8,128)(2,1)}), bf16[24,128,256]{2,1,0:T(8,128)(2,1)S(1)}, u32[]{:S(2)}, u32[]{:S(2)}) async-start(bf16[24,128,256]{2,1,0:T(8,128)(2,1)} %get-tuple-element.12), calls=%async_computation | async-start | bytes 3145728 | tf_op jit(solution)/shard_map/all_to_all | solution.py:293
  27.7 17.7 %copy-start.10 = (s32[1,1,3072,8]{2,3,1,0:T(8,128)S(1)}, s32[1,1,3072,8]{2,3,1,0:T(8,128)}, u32[]{:S(2)}) copy-start(s32[1,1,3072,8]{2,3,1,0:T(8,128)} %param.10) | copy-start | bytes 294916
  42.8 2.6 %copy-start.2 = (bf16[1024,3072]{1,0:T(8,128)(2,1)}, bf16[1024,3072]{1,0:T(8,128)(2,1)S(1)}, u32[]{:S(2)}) copy-start(bf16[1024,3072]{1,0:T(8,128)(2,1)S(1)} %shard_map.121.counts_ref) | copy-start | bytes 18874372
  75.5 4.5 %copy-start = (bf16[2048,3072]{1,0:T(8,128)(2,1)}, bf16[2048,3072]{1,0:T(8,128)(2,1)S(1)}, u32[]{:S(2)}) copy-start(bf16[2048,3072]{1,0:T(8,128)(2,1)S(1)} %shard_map.120.refs_2_.counts_ref) | copy-start | bytes 37748740
  85.4 2.8 %copy-start.3 = (bf16[1024,3072]{1,0:T(8,128)(2,1)S(1)}, bf16[1024,3072]{1,0:T(8,128)(2,1)}, u32[]{:S(2)}) copy-start(bf16[1024,3072]{1,0:T(8,128)(2,1)} %copy-done.2) | copy-start | bytes 18874372
  91.6 68.2 %all-to-all-start.1 = ((bf16[24,128,256]{2,1,0:T(8,128)(2,1)}), bf16[24,128,256]{2,1,0:T(8,128)(2,1)S(1)}, u32[]{:S(2)}, u32[]{:S(2)}) async-start(bf16[24,128,256]{2,1,0:T(8,128)(2,1)} %shard_map.123), calls=%async_computation.1 | async-start | bytes 3145728 | tf_op jit(solution)/shard_map/all_to_all | solution.py:300
  96.0 48.9 %reduce-scatter.2.cloned.1.call-start = ((), (), s32[]{:S(2)}) async-start(), calls=%async_computation.4 | async-start | bytes 1179648 | tf_op jit(solution)/shard_map/reduce_scatter | solution.py:302
  144.9 11.3 %collective-permute-start = (f32[128,256]{1,0:T(8,128)}, f32[128,256]{1,0:T(8,128)S(1)}, u32[]{:S(2)}, u32[]{:S(2)}) collective-permute-start(f32[128,256]{1,0:T(8,128)} %reduce-scatter.2.cloned.1.call-done.refs_0_), channel_id=1, source_target_pairs={{0,8},{8,16},{16,24},{24,0},{1,9},{9,17},{17,25},{25,1},{2,10},{10... | collective-permute-start | bytes 393224 | tf_op jit(solution)/shard_map/ppermute | solution.py:270
  148.1 8.6 %collective-permute-start.1 = (f32[128,256]{1,0:T(8,128)}, f32[128,256]{1,0:T(8,128)S(1)}, u32[]{:S(2)}, u32[]{:S(2)}) collective-permute-start(f32[128,256]{1,0:T(8,128)} %reduce-scatter.2.cloned.1.call-done.refs_0_), channel_id=1, source_target_pairs={{0,16},{8,24},{16,0},{24,8},{1,17},{9,25},{17,1},{25,9},{2,18},{10... | collective-permute-start | bytes 393224 | tf_op jit(solution)/shard_map/ppermute | solution.py:270
  152.7 7.1 %collective-permute-start.2 = (f32[128,256]{1,0:T(8,128)}, f32[128,256]{1,0:T(8,128)S(1)}, u32[]{:S(2)}, u32[]{:S(2)}) collective-permute-start(f32[128,256]{1,0:T(8,128)} %reduce-scatter.2.cloned.1.call-done.refs_0_), channel_id=1, source_target_pairs={{0,24},{8,0},{16,8},{24,16},{1,25},{9,1},{17,9},{25,17},{2,26},{10... | collective-permute-start | bytes 393224 | tf_op jit(solution)/shard_map/ppermute | solution.py:270
  159.8 4.6 %copy-start.1 = (bf16[2048,3072]{1,0:T(8,128)(2,1)S(1)}, bf16[2048,3072]{1,0:T(8,128)(2,1)}, u32[]{:S(2)}) copy-start(bf16[2048,3072]{1,0:T(8,128)(2,1)} %copy-done) | copy-start | bytes 37748740
  164.4 0.9 copy-start.6
  171.9 8.5 %copy-start.12 = (s32[1,32,1,64]{3,2,1,0:T(1,128)S(1)}, s32[1,32,1,64]{3,2,1,0:T(1,128)}, u32[]{:S(2)}) copy-start(s32[1,32,1,64]{3,2,1,0:T(1,128)} %param.11) | copy-start | bytes 24580
  171.9 45.6 %copy-start.4 = (f32[1,1024,256]{2,1,0:T(8,128)S(1)}, f32[1,1024,256]{2,1,0:T(8,128)}, u32[]{:S(2)}) copy-start(f32[1,1024,256]{2,1,0:T(8,128)} %param.16) | copy-start | bytes 3145732
  171.9 45.6 %copy-start.5 = (f32[1,512,256]{2,1,0:T(8,128)S(1)}, f32[1,512,256]{2,1,0:T(8,128)}, u32[]{:S(2)}) copy-start(f32[1,512,256]{2,1,0:T(8,128)} %param.14) | copy-start | bytes 1572868
  171.9 45.6 %copy-start.7 = (f32[1,1024]{1,0:T(1,128)S(1)}, f32[1,1024]{1,0:T(1,128)}, u32[]{:S(2)}) copy-start(f32[1,1024]{1,0:T(1,128)} %small_accum_ref.1) | copy-start | bytes 12292
  171.9 45.6 %copy-start.8 = (f32[1,512]{1,0:T(1,128)S(1)}, f32[1,512]{1,0:T(1,128)}, u32[]{:S(2)}) copy-start(f32[1,512]{1,0:T(1,128)} %giant_accum_ref.1) | copy-start | bytes 6148
  171.9 45.6 %all-to-all-start.2 = ((s16[32,208,128]{2,1,0:T(8,128)(2,1)}), s16[32,208,128]{2,1,0:T(8,128)(2,1)S(1)}, u32[]{:S(2)}, u32[]{:S(2)}) async-start(s16[32,208,128]{2,1,0:T(8,128)(2,1)} %shard_map.124), calls=%async_computation.3 | async-start | bytes 3407872 | tf_op jit(solution)/shard_map/all_to_all | solution.py:307
Sparse Core Ops, SparseCore 0:
  100.5 44.3 reduce-scatter.1

commit v3 on v2

--- a/solution.py
+++ b/solution.py
@@ -11,7 +11,7 @@
 TINY = 1e-08
 BF = jnp.bfloat16
 F32 = jnp.float32
-VMEM_LIMIT = 20 * 1024 * 1024
+VMEM_LIMIT = 48 * 1024 * 1024
 TAG_ROWS = 16
 
 
@@ -23,22 +23,22 @@
 def counts_kernel(ids_ref, out_ref):
     rows, samples = out_ref.shape
     bag = ids_ref.shape[0]
-    lanes = 256
+    lanes, tile = 256, 32
     first = pl.program_id(0) * rows
-    local = lax.broadcasted_iota(jnp.int32, (16, lanes), 0)
+    local = lax.broadcasted_iota(jnp.int32, (tile, lanes), 0)
 
     @pl.loop(0, samples // lanes)
     def _(chunk):
         at = pl.ds(pl.multiple_of(chunk * lanes, lanes), lanes)
-        named = [jnp.broadcast_to(ids_ref[k : k + 1, at], (16, lanes)) for k in range(bag)]
-
-        @pl.loop(0, rows // 16)
+        named = [jnp.broadcast_to(ids_ref[k : k + 1, at], (tile, lanes)) for k in range(bag)]
+
+        @pl.loop(0, rows // tile)
         def _(step):
-            bucket = local + (first + step * 16)
-            total = jnp.zeros((16, lanes), F32)
+            bucket = local + (first + step * tile)
+            total = jnp.zeros((tile, lanes), jnp.int32)
             for k in range(bag):
-                total = total + jnp.where(named[k] == bucket, 1.0, 0.0)
-            out_ref[pl.ds(pl.multiple_of(step * 16, 16), 16), at] = total.astype(BF)
+                total = total + jnp.where(named[k] == bucket, 1, 0)
+            out_ref[pl.ds(pl.multiple_of(step * tile, tile), tile), at] = total.astype(jnp.int8)
 
 
 def bag_counts(ids, buckets):
@@ -49,21 +49,31 @@
         grid=(buckets // rows,),
         in_specs=[pl.BlockSpec((bag, samples), lambda i: (0, 0))],
         out_specs=pl.BlockSpec((rows, samples), lambda i: (i, 0)),
-        out_shape=jax.ShapeDtypeStruct((buckets, samples), BF),
+        out_shape=jax.ShapeDtypeStruct((buckets, samples), jnp.int8),
         compiler_params=pltpu.CompilerParams(vmem_limit_bytes=VMEM_LIMIT),
         cost_estimate=pl.CostEstimate(
-            flops=3 * bag * buckets * samples, bytes_accessed=2 * buckets * samples, transcendentals=0
+            flops=3 * bag * buckets * samples, bytes_accessed=buckets * samples, transcendentals=0
         ),
     )(ids)
 
 
 def corner(array):
     lead = (1,) * (array.ndim - 2)
-    return pl.BlockSpec(lead + (16, 128), lambda *_: (0,) * array.ndim)
-
-
-def matmul_kernel(counts_ref, values_ref, out_ref):
-    out_ref[...] = jnp.dot(counts_ref[...], values_ref[...], preferred_element_type=F32)
+    return pl.BlockSpec(lead + (32, 128), lambda *_: (0,) * array.ndim)
+
+
+def split_kernel(place_ref, counts_ref, values_ref, *refs):
+    outs, sums = refs[:-1], refs[-1]
+    rows = counts_ref.shape[0]
+    at = pl.ds(pl.multiple_of(pl.program_id(0) * rows, rows), rows)
+    sums[at, :] = jnp.dot(counts_ref[...].astype(BF), values_ref[...], preferred_element_type=F32)
+
+    @pl.when(pl.program_id(0) == pl.num_programs(0) - 1)
+    def _():
+        piece = outs[0].shape[0]
+        for step, out_ref in enumerate(outs):
+            member = lax.rem(place_ref[0] + step, len(outs))
+            out_ref[...] = sums[pl.ds(pl.multiple_of(member * piece, piece), piece), :]
 
 
 def coded_rows(sums):
@@ -75,7 +85,7 @@
 
 def packed_kernel(capacity, place_ref, counts_ref, values_ref, *refs):
     terms, out_ref = refs[:-1], refs[-1]
-    sums = jnp.dot(counts_ref[...], values_ref[...], preferred_element_type=F32)
+    sums = jnp.dot(counts_ref[...].astype(BF), values_ref[...], preferred_element_type=F32)
     coded, power = coded_rows(sums)
     rows, width = sums.shape
     lanes = out_ref.shape[2]
@@ -100,27 +110,30 @@
         out_ref[block, first:, :] = tag.astype(jnp.int32).astype(jnp.int16)
 
 
-def bucket_sums(counts, values):
+def split_bucket_sums(counts, values, place, members):
     buckets, samples = counts.shape
     width = values.shape[1]
     rows = 512
-    return pl.pallas_call(
-        matmul_kernel,
+    piece = (buckets // members, width)
+    return pl.pallas_call(
+        split_kernel,
         grid=(buckets // rows,),
         in_specs=[
+            pl.BlockSpec(memory_space=pltpu.SMEM),
             pl.BlockSpec((rows, samples), lambda i: (i, 0)),
             pl.BlockSpec((samples, width), lambda i: (0, 0)),
         ],
-        out_specs=pl.BlockSpec((rows, width), lambda i: (i, 0)),
-        out_shape=jax.ShapeDtypeStruct((buckets, width), F32),
+        out_specs=[pl.BlockSpec(piece, lambda i: (0, 0))] * members,
+        out_shape=[jax.ShapeDtypeStruct(piece, F32)] * members,
+        scratch_shapes=[pltpu.VMEM((buckets, width), F32)],
         compiler_params=pltpu.CompilerParams(vmem_limit_bytes=VMEM_LIMIT),
-    )(counts, values)
+    )(place, counts, values)
 
 
 def packed_bucket_sums(counts, values, capacity, place, terms):
     buckets, samples = counts.shape
     width = values.shape[1]
-    rows, lanes = 512, 128
+    rows, lanes = 1024, 128
     mine = terms[0].shape[0] // len(terms)
     tall = (capacity + mine) * width // lanes + TAG_ROWS
     whole = pl.BlockSpec(terms[0].shape, lambda i: (0, 0))
@@ -263,12 +276,13 @@
     )(value, *others)
 
 
-def ring_terms(value, axis):
+def moved(value, axis, step):
     size = lax.axis_size(axis)
-    terms = [value]
-    for step in range(1, size):
-        terms.append(lax.ppermute(value, axis, [(i, (i + step) % size) for i in range(size)]))
-    return terms
+    return lax.ppermute(value, axis, [(i, (i + step) % size) for i in range(size)])
+
+
+def position(axis):
+    return lax.axis_index(axis).astype(jnp.int32).reshape(1)
 
 
 def body(
@@ -294,16 +308,14 @@
     lengths = bag_lengths[0, 0]
     small_counts = bag_counts(masked_ids(small_ids[0, 0], lengths[:, 1]), small_weight.shape[1])
     giant_counts = bag_counts(masked_ids(giant_slot[0, 0], lengths[:, 0]), groups * capacity)
-    small_sum = bucket_sums(small_counts, small_values.reshape(samples, width))
-
-    giant_out = after(pairs[:, :, 0, :].transpose(1, 0, 2), small_sum, giant_counts)
+    giant_out = after(pairs[:, :, 0, :].transpose(1, 0, 2), small_values, small_counts, giant_counts)
     giant_values = exchange(giant_out, "col").reshape(samples, width)
 
-    small_sum = lax.psum_scatter(small_sum, "rep", scatter_dimension=0, tiled=True)
-    terms = ring_terms(small_sum, "row")
-    place = lax.axis_index("row").astype(jnp.int32).reshape(1)
-
-    packed = packed_bucket_sums(giant_counts, giant_values, capacity, place, terms)
+    pieces = split_bucket_sums(small_counts, small_values.reshape(samples, width), position("rep"), lax.axis_size("rep"))
+    small_sum = sum(moved(piece, "rep", step) if step else piece for step, piece in enumerate(pieces))
+    terms = [moved(small_sum, "row", step) if step else small_sum for step in range(lax.axis_size("row"))]
+
+    packed = packed_bucket_sums(giant_counts, giant_values, capacity, position("row"), terms)
     arrived = exchange(packed, ("row", "rep"))
     targets = touched_rows[0, :, 0, :].reshape(1, -1)
     new_gw, new_ga, new_sw, new_sa = update(

time: 231 us -> 212 us (0.918)
  starting transfers between devices: 39 us -> 68.2 us
  waiting for transfers between devices: 94.2 us -> 74.5 us
  between operations: 14.2 us -> 0.91 us
  local copies, waits for them, and re-layouts: 21 us -> 9.92 us
  Pallas kernels: 61.3 us -> 56.4 us
    reduce_scatter x1 -> x0, waiting for transfers between devices: 48.1 us -> none  [body(): lax.psum_scatter(small_sum, 'rep', scatter_dimension=0, tiled=True)]
    ppermute x3 -> x10, starting transfers between devices: 11.3 us -> 39.6 us  [moved(): lax.ppermute(value, axis, [(i, (i + step) % size) for i in range(size)])]
    ppermute x3 -> x10, waiting for transfers between devices: 3.65 us -> 16.6 us  [moved(): lax.ppermute(value, axis, [(i, (i + step) % size) for i in range(size)])]
    all_to_all x1, waiting for transfers between devices: 5.37 us -> 17.7 us  [body(): small_values = exchange(pairs[:, :, 1, :].transpose(1, 0, 2), 'col')]
    unnamed x28 -> x26, local copies, waits for them, and re-layouts: 18.9 us -> 7.8 us
    pallas_call x2, Pallas kernels: 45.1 us -> 38.2 us  [bag_counts(): pl.pallas_call(counts_kernel, grid=(buckets // rows,), in_specs=[pl.Block...]
    all_to_all x1, waiting for transfers between devices: 36.4 us -> 40.2 us  [body(): arrived = exchange(packed, ('row', 'rep'))]
    pallas_call x1, Pallas kernels: 6.59 us -> 9.42 us  [packed_bucket_sums(): pl.pallas_call(functools.partial(packed_kernel, capacity), grid=(buckets...]
  transfers between devices with their start and end apart: 7 -> 13, of which waited for: 5 -> 8; matrix products, arithmetic and copies ran while one was open for 1% -> 1% of each run, Pallas kernels for 20% -> 19%
where the time goes in v3:
time: 212 us; the launch traced here: 211 us
  waiting for transfers between devices  74.5 us (35%)
  starting transfers between devices  68.2 us (32%)
  Pallas kernels  56.4 us (27%)
  local copies, waits for them, and re-layouts  9.92 us (5%)
    all_to_all x1, waiting for transfers between devices, body(): arrived = exchange(packed, ('row', 'rep'))  40.2 us
    ppermute x10, starting transfers between devices, moved(): lax.ppermute(value, axis, [(i, (i + step) % size) for i in range(size)])  39.6 us
    pallas_call x2, Pallas kernels, bag_counts(): pl.pallas_call(counts_kernel, grid=(buckets // rows,), in_specs=[pl.Block...  38.2 us
    all_to_all x1, waiting for transfers between devices, body(): small_values = exchange(pairs[:, :, 1, :].transpose(1, 0, 2), 'col')  17.7 us
    ppermute x10, waiting for transfers between devices, moved(): lax.ppermute(value, axis, [(i, (i + step) % size) for i in range(size)])  16.6 us
    all_to_all x1, starting transfers between devices, body(): small_values = exchange(pairs[:, :, 1, :].transpose(1, 0, 2), 'col')  15.5 us
    pallas_call x1, Pallas kernels, packed_bucket_sums(): pl.pallas_call(functools.partial(packed_kernel, capacity), grid=(buckets...  9.42 us
    all_to_all x1, starting transfers between devices, body(): arrived = exchange(packed, ('row', 'rep'))  8.05 us
  transfers between devices with their start and end apart: 13, of which 8 were waited for; matrix products, arithmetic and copies ran while one was open for 1% of the time, Pallas kernels for 19%

profile of v3, /device:TPU:8, one launch (start us, length us, event | category | flops | bytes accessed | tf_op | source)
XLA Modules:
  0.0 210.8 jit_solution(2916722863203396617)
XLA Ops:
  0.6 3.0 %copy.14 = bf16[1,128,48,256]{3,1,2,0:T(8,128)(2,1)S(1)} copy(bf16[1,128,48,256]{3,2,1,0:T(8,128)(2,1)} %param.9) | data formatting | bytes 6291456 | tf_op args[0]
  3.6 2.0 slice_bitcast_fusion
  5.6 0.0 copy-start.10
  5.6 0.0 copy-start.8
  5.6 15.5 %all-to-all-start = ((bf16[24,128,256]{2,1,0:T(8,128)(2,1)}), bf16[24,128,256]{2,1,0:T(8,128)(2,1)S(1)}, u32[]{:S(2)}, u32[]{:S(2)}) async-start(bf16[24,128,256]{2,1,0:T(8,128)(2,1)} %get-tuple-element.28), calls=%async_computation | async-start | bytes 3145728 | tf_op jit(solution)/shard_map/all_to_all | solution.py:307
  21.2 0.0 copy-done.10
  21.2 0.0 copy-done.8
  21.2 0.0 copy-start.9
  21.2 12.4 %shard_map.121.refs_2_.counts_ref = s8[1024,3072]{1,0:T(32,128)(4,1)S(1)} custom-call(s32[8,3072]{1,0:T(8,128)S(1)} %fusion.ids_ref), custom_call_target="tpu_custom_call" | custom-call | flops 75497472 | bytes 3145728 | tf_op jit(solution)/shard_map/pallas_call | solution.py:47
  33.7 0.0 copy-start
  33.7 1.7 copy-done
  35.4 0.0 copy-done.9
  35.4 25.7 %shard_map.120.refs_3_.counts_ref = s8[2048,3072]{1,0:T(32,128)(4,1)} custom-call(s32[8,3072]{1,0:T(8,128)S(1)} %fusion.1.ids_ref), custom_call_target="tpu_custom_call" | custom-call | flops 150994944 | bytes 6291456 | tf_op jit(solution)/shard_map/pallas_call | solution.py:47
  61.1 17.7 %all-to-all-done.refs_1_ = bf16[24,128,256]{2,1,0:T(8,128)(2,1)S(1)} async-done(((bf16[24,128,256]{2,1,0:T(8,128)(2,1)}), bf16[24,128,256]{2,1,0:T(8,128)(2,1)S(1)}, u32[]{:S(2)}, u32[]{:S(2)}) %all-to-all-start) | async-done | bytes 1572896 | tf_op jit(solution)/shard_map/all_to_all | solution.py:307
  78.9 0.0 copy-start.2
  78.9 1.2 copy-done.2
  80.0 0.7 shard_map.122
  80.7 0.0 copy-start.1
  80.7 5.0 %all-to-all-start.1 = ((bf16[24,128,256]{2,1,0:T(8,128)(2,1)}), bf16[24,128,256]{2,1,0:T(8,128)(2,1)}, u32[]{:S(2)}, u32[]{:S(2)}) async-start(bf16[24,128,256]{2,1,0:T(8,128)(2,1)} %shard_map.122), calls=%async_computation.1 | async-start | bytes 3145728 | tf_op jit(solution)/shard_map/all_to_all | solution.py:312
  85.7 0.0 copy-done.1
  85.7 0.0 copy-start.3
  85.7 1.4 copy-done.3
  87.1 2.0 shard_map.123
  89.2 2.4 %collective-permute-start.6 = (f32[128,256]{1,0:T(8,128)S(1)}, f32[128,256]{1,0:T(8,128)S(1)}, u32[]{:S(2)}, u32[]{:S(2)}) collective-permute-start(f32[128,256]{1,0:T(8,128)S(1)} %get-tuple-element.23), channel_id=1, source_target_pairs={{0,7},{1,0},{2,1},{3,2},{4,3},{5,4},{6,5},{7,6},{8,15},{9,8},{10,9... | collective-permute-start | bytes 393224 | tf_op jit(solution)/shard_map/ppermute | solution.py:281
  91.5 6.2 %collective-permute-start.5 = (f32[128,256]{1,0:T(8,128)S(1)}, f32[128,256]{1,0:T(8,128)S(1)}, u32[]{:S(2)}, u32[]{:S(2)}) collective-permute-start(f32[128,256]{1,0:T(8,128)S(1)} %get-tuple-element.22), channel_id=1, source_target_pairs={{0,6},{1,7},{2,0},{3,1},{4,2},{5,3},{6,4},{7,5},{8,14},{9,15},{10,... | collective-permute-start | bytes 393224 | tf_op jit(solution)/shard_map/ppermute | solution.py:281
  97.7 3.9 %collective-permute-start.4 = (f32[128,256]{1,0:T(8,128)S(1)}, f32[128,256]{1,0:T(8,128)S(1)}, u32[]{:S(2)}, u32[]{:S(2)}) collective-permute-start(f32[128,256]{1,0:T(8,128)S(1)} %get-tuple-element.21), channel_id=1, source_target_pairs={{0,5},{1,6},{2,7},{3,0},{4,1},{5,2},{6,3},{7,4},{8,13},{9,14},{10,... | collective-permute-start | bytes 393224 | tf_op jit(solution)/shard_map/ppermute | solution.py:281
  101.6 5.0 %collective-permute-start.3 = (f32[128,256]{1,0:T(8,128)S(1)}, f32[128,256]{1,0:T(8,128)S(1)}, u32[]{:S(2)}, u32[]{:S(2)}) collective-permute-start(f32[128,256]{1,0:T(8,128)S(1)} %get-tuple-element.20), channel_id=1, source_target_pairs={{0,4},{1,5},{2,6},{3,7},{4,0},{5,1},{6,2},{7,3},{8,12},{9,13},{10,... | collective-permute-start | bytes 393224 | tf_op jit(solution)/shard_map/ppermute | solution.py:281
  106.7 3.7 %collective-permute-start.2 = (f32[128,256]{1,0:T(8,128)S(1)}, f32[128,256]{1,0:T(8,128)S(1)}, u32[]{:S(2)}, u32[]{:S(2)}) collective-permute-start(f32[128,256]{1,0:T(8,128)S(1)} %get-tuple-element.19), channel_id=1, source_target_pairs={{0,3},{1,4},{2,5},{3,6},{4,7},{5,0},{6,1},{7,2},{8,11},{9,12},{10,... | collective-permute-start | bytes 393224 | tf_op jit(solution)/shard_map/ppermute | solution.py:281
  110.4 0.0 collective-permute-done.6
  110.4 4.5 %collective-permute-start.1 = (f32[128,256]{1,0:T(8,128)S(1)}, f32[128,256]{1,0:T(8,128)S(1)}, u32[]{:S(2)}, u32[]{:S(2)}) collective-permute-start(f32[128,256]{1,0:T(8,128)S(1)} %get-tuple-element.18), channel_id=1, source_target_pairs={{0,2},{1,3},{2,4},{3,5},{4,6},{5,7},{6,0},{7,1},{8,10},{9,11},{10,... | collective-permute-start | bytes 393224 | tf_op jit(solution)/shard_map/ppermute | solution.py:281
  114.9 0.0 collective-permute-done.5
  114.9 2.6 %collective-permute-start = (f32[128,256]{1,0:T(8,128)S(1)}, f32[128,256]{1,0:T(8,128)S(1)}, u32[]{:S(2)}, u32[]{:S(2)}) collective-permute-start(f32[128,256]{1,0:T(8,128)S(1)} %get-tuple-element.17), channel_id=1, source_target_pairs={{0,1},{1,2},{2,3},{3,4},{4,5},{5,6},{6,7},{7,0},{8,9},{9,10},{10,1... | collective-permute-start | bytes 393224 | tf_op jit(solution)/shard_map/ppermute | solution.py:281
  117.5 0.0 collective-permute-done.4
  117.5 3.0 %collective-permute-done.3 = f32[128,256]{1,0:T(8,128)S(1)} collective-permute-done((f32[128,256]{1,0:T(8,128)S(1)}, f32[128,256]{1,0:T(8,128)S(1)}, u32[]{:S(2)}, u32[]{:S(2)}) %collective-permute-start.3) | collective-permute-done | bytes 131104 | tf_op jit(solution)/shard_map/ppermute | solution.py:281
  120.5 3.4 %collective-permute-done.2 = f32[128,256]{1,0:T(8,128)S(1)} collective-permute-done((f32[128,256]{1,0:T(8,128)S(1)}, f32[128,256]{1,0:T(8,128)S(1)}, u32[]{:S(2)}, u32[]{:S(2)}) %collective-permute-start.2) | collective-permute-done | bytes 131104 | tf_op jit(solution)/shard_map/ppermute | solution.py:281
  123.9 5.2 %collective-permute-done.1 = f32[128,256]{1,0:T(8,128)S(1)} collective-permute-done((f32[128,256]{1,0:T(8,128)S(1)}, f32[128,256]{1,0:T(8,128)S(1)}, u32[]{:S(2)}, u32[]{:S(2)}) %collective-permute-start.1) | collective-permute-done | bytes 131104 | tf_op jit(solution)/shard_map/ppermute | solution.py:281
  129.1 1.5 collective-permute-done
  130.6 0.1 add_add_fusion.refs_0_
  130.7 3.4 %collective-permute-start.7 = (f32[128,256]{1,0:T(8,128)S(1)}, f32[128,256]{1,0:T(8,128)S(1)}, u32[]{:S(2)}, u32[]{:S(2)}) collective-permute-start(f32[128,256]{1,0:T(8,128)S(1)} %add_add_fusion.refs_0_), channel_id=1, source_target_pairs={{0,8},{8,16},{16,24},{24,0},{1,9},{9,17},{17,25},{25,1},{2,10},{10... | collective-permute-start | bytes 393224 | tf_op jit(solution)/shard_map/ppermute | solution.py:281
  134.1 4.6 %collective-permute-start.8 = (f32[128,256]{1,0:T(8,128)S(1)}, f32[128,256]{1,0:T(8,128)S(1)}, u32[]{:S(2)}, u32[]{:S(2)}) collective-permute-start(f32[128,256]{1,0:T(8,128)S(1)} %add_add_fusion.refs_0_), channel_id=1, source_target_pairs={{0,16},{8,24},{16,0},{24,8},{1,17},{9,25},{17,1},{25,9},{2,18},{10... | collective-permute-start | bytes 393224 | tf_op jit(solution)/shard_map/ppermute | solution.py:281
  138.7 3.3 %collective-permute-start.9 = (f32[128,256]{1,0:T(8,128)S(1)}, f32[128,256]{1,0:T(8,128)S(1)}, u32[]{:S(2)}, u32[]{:S(2)}) collective-permute-start(f32[128,256]{1,0:T(8,128)S(1)} %add_add_fusion.refs_0_), channel_id=1, source_target_pairs={{0,24},{8,0},{16,8},{24,16},{1,25},{9,1},{17,9},{25,17},{2,26},{10... | collective-permute-start | bytes 393224 | tf_op jit(solution)/shard_map/ppermute | solution.py:281
  142.1 0.0 collective-permute-done.7.refs_1_
  142.1 0.4 collective-permute-done.8.refs_2_
  142.6 3.0 %collective-permute-done.9.refs_3_ = f32[128,256]{1,0:T(8,128)S(1)} collective-permute-done((f32[128,256]{1,0:T(8,128)S(1)}, f32[128,256]{1,0:T(8,128)S(1)}, u32[]{:S(2)}, u32[]{:S(2)}) %collective-permute-start.9) | collective-permute-done | bytes 131104 | tf_op jit(solution)/shard_map/ppermute | solution.py:281
  145.6 0.0 all-to-all-done.1
  145.6 9.4 %shard_map.124 = s16[32,208,128]{2,1,0:T(8,128)(2,1)} custom-call(s32[1]{0:T(128)} %bitcast.place_ref, s8[2048,3072]{1,0:T(32,128)(4,1)} %shard_map.120.refs_3_.counts_ref, bf16[3072,256]{1,0:T(8,128)(2,1)} %bitcast.13.values_ref, f32[128,256]{1,0:T(8,128)S(1)} %add_add_fusion.refs_0_, f32[128,256]{1,0:T(8,128)S(1)} %collective-permute-done.7.refs_1_, ...), custom_call_target="tpu_custom_call" | custom-call | tf_op jit(solution)/shard_map/pallas_call | solution.py:140
  155.0 0.0 copy-start.11
  155.0 0.0 copy-start.4
  155.0 0.0 copy-start.5
  155.0 0.0 copy-start.6
  155.1 0.0 copy-start.7
  155.1 8.1 %all-to-all-start.2 = ((s16[32,208,128]{2,1,0:T(8,128)(2,1)}), s16[32,208,128]{2,1,0:T(8,128)(2,1)S(1)}, u32[]{:S(2)}, u32[]{:S(2)}) async-start(s16[32,208,128]{2,1,0:T(8,128)(2,1)} %shard_map.124), calls=%async_computation.2 | async-start | bytes 3407872 | tf_op jit(solution)/shard_map/all_to_all | solution.py:319
  163.1 0.5 broadcast.3
  163.6 0.0 copy-done.11
  163.6 0.7 reduce.3
  164.3 0.1 reshape_squeeze.6.targets_ref
  164.4 40.2 %all-to-all-done.2.arrived_ref = s16[32,208,128]{2,1,0:T(8,128)(2,1)S(1)} async-done(((s16[32,208,128]{2,1,0:T(8,128)(2,1)}), s16[32,208,128]{2,1,0:T(8,128)(2,1)S(1)}, u32[]{:S(2)}, u32[]{:S(2)}) %all-to-all-start.2) | async-done | bytes 1703968 | tf_op jit(solution)/shard_map/all_to_all | solution.py:319
  204.6 0.0 copy-done.4
  204.6 0.0 copy-done.5
  204.6 0.0 copy-done.6
  204.6 0.0 copy-done.7
  204.6 6.1 %shard_map.125 = (f32[512,256]{1,0:T(8,128)}, f32[1,512]{1,0:T(1,128)}, f32[1024,256]{1,0:T(8,128)}, f32[1,1024]{1,0:T(1,128)}) custom-call(s32[1,2048]{1,0:T(1,128)S(1)} %reshape_squeeze.6.targets_ref, s16[32,208,128]{2,1,0:T(8,128)(2,1)S(1)} %all-to-all-done.2.arrived_ref, f32[512,256]{1,0:T(8,128)S(1)} %bitcast.38, f32[1,512]{1,0:T(1,128)S(1)} %copy-done.7, ...), custom_call_target="tpu_custom_call" | custom-call | tf_op jit(solution)/shard_map/pallas_call | solution.py:247
  (3 shorter events, 0.1 us)
Async XLA Ops:
  5.6 15.5 %copy-start.10 = (s32[1,1,3072,2]{2,3,1,0:T(2,128)S(1)}, s32[1,1,3072,2]{2,3,1,0:T(2,128)}, u32[]{:S(2)}) copy-start(s32[1,1,3072,2]{2,3,1,0:T(2,128)} %param.12) | copy-start | bytes 73732
  5.6 15.6 %copy-start.8 = (s32[1,1,3072,8]{2,3,1,0:T(8,128)S(1)}, s32[1,1,3072,8]{2,3,1,0:T(8,128)}, u32[]{:S(2)}) copy-start(s32[1,1,3072,8]{2,3,1,0:T(8,128)} %param.13) | copy-start | bytes 294916
  5.6 73.2 %all-to-all-start = ((bf16[24,128,256]{2,1,0:T(8,128)(2,1)}), bf16[24,128,256]{2,1,0:T(8,128)(2,1)S(1)}, u32[]{:S(2)}, u32[]{:S(2)}) async-start(bf16[24,128,256]{2,1,0:T(8,128)(2,1)} %get-tuple-element.28), calls=%async_computation | async-start | bytes 3145728 | tf_op jit(solution)/shard_map/all_to_all | solution.py:307
  21.2 14.2 %copy-start.9 = (s32[1,1,3072,8]{2,3,1,0:T(8,128)S(1)}, s32[1,1,3072,8]{2,3,1,0:T(8,128)}, u32[]{:S(2)}) copy-start(s32[1,1,3072,8]{2,3,1,0:T(8,128)} %param.10) | copy-start | bytes 294916
  33.7 1.7 copy-start
  78.9 1.2 copy-start.2
  80.7 5.0 %copy-start.1 = (s8[1024,3072]{1,0:T(32,128)(4,1)S(1)}, s8[1024,3072]{1,0:T(32,128)(4,1)}, u32[]{:S(2)}) copy-start(s8[1024,3072]{1,0:T(32,128)(4,1)} %copy-done) | copy-start | bytes 9437188
  80.7 64.9 %all-to-all-start.1 = ((bf16[24,128,256]{2,1,0:T(8,128)(2,1)}), bf16[24,128,256]{2,1,0:T(8,128)(2,1)}, u32[]{:S(2)}, u32[]{:S(2)}) async-start(bf16[24,128,256]{2,1,0:T(8,128)(2,1)} %shard_map.122), calls=%async_computation.1 | async-start | bytes 3145728 | tf_op jit(solution)/shard_map/all_to_all | solution.py:312
  85.7 1.4 copy-start.3
  89.2 21.2 %collective-permute-start.6 = (f32[128,256]{1,0:T(8,128)S(1)}, f32[128,256]{1,0:T(8,128)S(1)}, u32[]{:S(2)}, u32[]{:S(2)}) collective-permute-start(f32[128,256]{1,0:T(8,128)S(1)} %get-tuple-element.23), channel_id=1, source_target_pairs={{0,7},{1,0},{2,1},{3,2},{4,3},{5,4},{6,5},{7,6},{8,15},{9,8},{10,9... | collective-permute-start | bytes 393224 | tf_op jit(solution)/shard_map/ppermute | solution.py:281
  91.5 23.4 %collective-permute-start.5 = (f32[128,256]{1,0:T(8,128)S(1)}, f32[128,256]{1,0:T(8,128)S(1)}, u32[]{:S(2)}, u32[]{:S(2)}) collective-permute-start(f32[128,256]{1,0:T(8,128)S(1)} %get-tuple-element.22), channel_id=1, source_target_pairs={{0,6},{1,7},{2,0},{3,1},{4,2},{5,3},{6,4},{7,5},{8,14},{9,15},{10,... | collective-permute-start | bytes 393224 | tf_op jit(solution)/shard_map/ppermute | solution.py:281
  97.7 19.8 %collective-permute-start.4 = (f32[128,256]{1,0:T(8,128)S(1)}, f32[128,256]{1,0:T(8,128)S(1)}, u32[]{:S(2)}, u32[]{:S(2)}) collective-permute-start(f32[128,256]{1,0:T(8,128)S(1)} %get-tuple-element.21), channel_id=1, source_target_pairs={{0,5},{1,6},{2,7},{3,0},{4,1},{5,2},{6,3},{7,4},{8,13},{9,14},{10,... | collective-permute-start | bytes 393224 | tf_op jit(solution)/shard_map/ppermute | solution.py:281
  101.6 18.9 %collective-permute-start.3 = (f32[128,256]{1,0:T(8,128)S(1)}, f32[128,256]{1,0:T(8,128)S(1)}, u32[]{:S(2)}, u32[]{:S(2)}) collective-permute-start(f32[128,256]{1,0:T(8,128)S(1)} %get-tuple-element.20), channel_id=1, source_target_pairs={{0,4},{1,5},{2,6},{3,7},{4,0},{5,1},{6,2},{7,3},{8,12},{9,13},{10,... | collective-permute-start | bytes 393224 | tf_op jit(solution)/shard_map/ppermute | solution.py:281
  106.7 17.2 %collective-permute-start.2 = (f32[128,256]{1,0:T(8,128)S(1)}, f32[128,256]{1,0:T(8,128)S(1)}, u32[]{:S(2)}, u32[]{:S(2)}) collective-permute-start(f32[128,256]{1,0:T(8,128)S(1)} %get-tuple-element.19), channel_id=1, source_target_pairs={{0,3},{1,4},{2,5},{3,6},{4,7},{5,0},{6,1},{7,2},{8,11},{9,12},{10,... | collective-permute-start | bytes 393224 | tf_op jit(solution)/shard_map/ppermute | solution.py:281
  110.4 18.7 %collective-permute-start.1 = (f32[128,256]{1,0:T(8,128)S(1)}, f32[128,256]{1,0:T(8,128)S(1)}, u32[]{:S(2)}, u32[]{:S(2)}) collective-permute-start(f32[128,256]{1,0:T(8,128)S(1)} %get-tuple-element.18), channel_id=1, source_target_pairs={{0,2},{1,3},{2,4},{3,5},{4,6},{5,7},{6,0},{7,1},{8,10},{9,11},{10,... | collective-permute-start | bytes 393224 | tf_op jit(solution)/shard_map/ppermute | solution.py:281
  114.9 15.7 %collective-permute-start = (f32[128,256]{1,0:T(8,128)S(1)}, f32[128,256]{1,0:T(8,128)S(1)}, u32[]{:S(2)}, u32[]{:S(2)}) collective-permute-start(f32[128,256]{1,0:T(8,128)S(1)} %get-tuple-element.17), channel_id=1, source_target_pairs={{0,1},{1,2},{2,3},{3,4},{4,5},{5,6},{6,7},{7,0},{8,9},{9,10},{10,1... | collective-permute-start | bytes 393224 | tf_op jit(solution)/shard_map/ppermute | solution.py:281
  130.7 11.4 %collective-permute-start.7 = (f32[128,256]{1,0:T(8,128)S(1)}, f32[128,256]{1,0:T(8,128)S(1)}, u32[]{:S(2)}, u32[]{:S(2)}) collective-permute-start(f32[128,256]{1,0:T(8,128)S(1)} %add_add_fusion.refs_0_), channel_id=1, source_target_pairs={{0,8},{8,16},{16,24},{24,0},{1,9},{9,17},{17,25},{25,1},{2,10},{10... | collective-permute-start | bytes 393224 | tf_op jit(solution)/shard_map/ppermute | solution.py:281
  134.1 8.5 %collective-permute-start.8 = (f32[128,256]{1,0:T(8,128)S(1)}, f32[128,256]{1,0:T(8,128)S(1)}, u32[]{:S(2)}, u32[]{:S(2)}) collective-permute-start(f32[128,256]{1,0:T(8,128)S(1)} %add_add_fusion.refs_0_), channel_id=1, source_target_pairs={{0,16},{8,24},{16,0},{24,8},{1,17},{9,25},{17,1},{25,9},{2,18},{10... | collective-permute-start | bytes 393224 | tf_op jit(solution)/shard_map/ppermute | solution.py:281
  138.7 6.9 %collective-permute-start.9 = (f32[128,256]{1,0:T(8,128)S(1)}, f32[128,256]{1,0:T(8,128)S(1)}, u32[]{:S(2)}, u32[]{:S(2)}) collective-permute-start(f32[128,256]{1,0:T(8,128)S(1)} %add_add_fusion.refs_0_), channel_id=1, source_target_pairs={{0,24},{8,0},{16,8},{24,16},{1,25},{9,1},{17,9},{25,17},{2,26},{10... | collective-permute-start | bytes 393224 | tf_op jit(solution)/shard_map/ppermute | solution.py:281
  155.0 8.6 %copy-start.11 = (s32[1,32,1,64]{3,2,1,0:T(1,128)S(1)}, s32[1,32,1,64]{3,2,1,0:T(1,128)}, u32[]{:S(2)}) copy-start(s32[1,32,1,64]{3,2,1,0:T(1,128)} %param.11) | copy-start | bytes 24580
  155.0 49.6 %copy-start.4 = (f32[1,1024,256]{2,1,0:T(8,128)S(1)}, f32[1,1024,256]{2,1,0:T(8,128)}, u32[]{:S(2)}) copy-start(f32[1,1024,256]{2,1,0:T(8,128)} %param.16) | copy-start | bytes 3145732
  155.0 49.6 %copy-start.5 = (f32[1,512,256]{2,1,0:T(8,128)S(1)}, f32[1,512,256]{2,1,0:T(8,128)}, u32[]{:S(2)}) copy-start(f32[1,512,256]{2,1,0:T(8,128)} %param.14) | copy-start | bytes 1572868
  155.0 49.6 %copy-start.6 = (f32[1,1024]{1,0:T(1,128)S(1)}, f32[1,1024]{1,0:T(1,128)}, u32[]{:S(2)}) copy-start(f32[1,1024]{1,0:T(1,128)} %small_accum_ref.1) | copy-start | bytes 12292
  155.1 49.6 %copy-start.7 = (f32[1,512]{1,0:T(1,128)S(1)}, f32[1,512]{1,0:T(1,128)}, u32[]{:S(2)}) copy-start(f32[1,512]{1,0:T(1,128)} %giant_accum_ref.1) | copy-start | bytes 6148
  155.1 49.5 %all-to-all-start.2 = ((s16[32,208,128]{2,1,0:T(8,128)(2,1)}), s16[32,208,128]{2,1,0:T(8,128)(2,1)S(1)}, u32[]{:S(2)}, u32[]{:S(2)}) async-start(s16[32,208,128]{2,1,0:T(8,128)(2,1)} %shard_map.124), calls=%async_computation.2 | async-start | bytes 3407872 | tf_op jit(solution)/shard_map/all_to_all | solution.py:319

commit v4 on v3

--- a/solution.py
+++ b/solution.py
@@ -62,6 +62,13 @@
     return pl.BlockSpec(lead + (32, 128), lambda *_: (0,) * array.ndim)
 
 
+def cut(sums, place, outs):
+    piece = outs[0].shape[0]
+    for step, out_ref in enumerate(outs):
+        member = lax.rem(place + step, len(outs))
+        out_ref[...] = sums[pl.ds(pl.multiple_of(member * piece, piece), piece), :]
+
+
 def split_kernel(place_ref, counts_ref, values_ref, *refs):
     outs, sums = refs[:-1], refs[-1]
     rows = counts_ref.shape[0]
@@ -70,10 +77,16 @@
 
     @pl.when(pl.program_id(0) == pl.num_programs(0) - 1)
     def _():
-        piece = outs[0].shape[0]
-        for step, out_ref in enumerate(outs):
-            member = lax.rem(place_ref[0] + step, len(outs))
-            out_ref[...] = sums[pl.ds(pl.multiple_of(member * piece, piece), piece), :]
+        cut(sums, place_ref[0], outs)
+
+
+def halves_kernel(count, distance, place_ref, *refs):
+    terms, outs, sums = refs[:count], refs[count:-1], refs[-1]
+    total = terms[0][...]
+    for term in terms[1:]:
+        total = total + term[...]
+    sums[...] = total
+    cut(sums, lax.div(place_ref[0], distance), outs)
 
 
 def coded_rows(sums):
@@ -83,17 +96,16 @@
     return coded.astype(jnp.int32).astype(jnp.int16), power
 
 
-def packed_kernel(capacity, place_ref, counts_ref, values_ref, *refs):
+def packed_kernel(capacity, counts_ref, values_ref, *refs):
     terms, out_ref = refs[:-1], refs[-1]
     sums = jnp.dot(counts_ref[...].astype(BF), values_ref[...], preferred_element_type=F32)
     coded, power = coded_rows(sums)
     rows, width = sums.shape
     lanes = out_ref.shape[2]
-    mine = terms[0].shape[0] // len(terms)
-    at = pl.ds(pl.multiple_of(place_ref[0] * mine, mine), mine)
-    small = terms[0][at, :]
+    mine = terms[0].shape[0]
+    small = terms[0][...]
     for term in terms[1:]:
-        small = small + term[at, :]
+        small = small + term[...]
     small_coded, small_power = coded_rows(small)
     tall = capacity + mine
     diagonal = lax.broadcasted_iota(jnp.int32, (tall, lanes), 0) == lax.broadcasted_iota(jnp.int32, (tall, lanes), 1)
@@ -130,18 +142,30 @@
     )(place, counts, values)
 
 
-def packed_bucket_sums(counts, values, capacity, place, terms):
+def split_halves(terms, place, distance):
+    rows, width = terms[0].shape
+    piece = (rows // 2, width)
+    return pl.pallas_call(
+        functools.partial(halves_kernel, len(terms), distance),
+        in_specs=[pl.BlockSpec(memory_space=pltpu.SMEM)] + [pl.BlockSpec(memory_space=pltpu.VMEM)] * len(terms),
+        out_specs=[pl.BlockSpec(memory_space=pltpu.VMEM)] * 2,
+        out_shape=[jax.ShapeDtypeStruct(piece, F32)] * 2,
+        scratch_shapes=[pltpu.VMEM((rows, width), F32)],
+        compiler_params=pltpu.CompilerParams(vmem_limit_bytes=VMEM_LIMIT),
+    )(place, *terms)
+
+
+def packed_bucket_sums(counts, values, capacity, terms):
     buckets, samples = counts.shape
     width = values.shape[1]
-    rows, lanes = 1024, 128
-    mine = terms[0].shape[0] // len(terms)
+    rows, lanes = 512, 128
+    mine = terms[0].shape[0]
     tall = (capacity + mine) * width // lanes + TAG_ROWS
     whole = pl.BlockSpec(terms[0].shape, lambda i: (0, 0))
     return pl.pallas_call(
         functools.partial(packed_kernel, capacity),
         grid=(buckets // rows,),
         in_specs=[
-            pl.BlockSpec(memory_space=pltpu.SMEM),
             pl.BlockSpec((rows, samples), lambda i: (i, 0)),
             pl.BlockSpec((samples, width), lambda i: (0, 0)),
         ]
@@ -149,7 +173,7 @@
         out_specs=pl.BlockSpec((rows // capacity, tall, lanes), lambda i: (i, 0, 0)),
         out_shape=jax.ShapeDtypeStruct((buckets // capacity, tall, lanes), jnp.int16),
         compiler_params=pltpu.CompilerParams(vmem_limit_bytes=VMEM_LIMIT),
-    )(place, counts, values, *terms)
+    )(counts, values, *terms)
 
 
 def adagrad_step(weight, accum, grad):
@@ -166,7 +190,6 @@
 
 def update_kernel(
     capacity,
-    outer,
     targets_ref,
     arrived_ref,
     giant_weight_ref,
@@ -212,14 +235,13 @@
     new_giant_weight_ref[...] = new_weight
     new_giant_accum_ref[...] = new_accum
 
-    band = outer * mine
-    inner = groups // outer
-    bands = small_weight_ref.shape[0] // band
-    for local in range(bands):
-        at = slice(local * band, (local + 1) * band)
+    band = lanes // mine
+    local_groups = small_weight_ref.shape[0] // mine
+    for local in range(0, local_groups, band):
+        at = slice(local * mine, (local + band) * mine)
         pieces = []
-        for place in range(outer):
-            group = place * inner + pl.program_id(0) * bands + local
+        for place in range(band):
+            group = pl.program_id(0) * local_groups + local + place
             scale = scales(group)[capacity : capacity + mine]
             pair = []
             for part in range(halves):
@@ -232,11 +254,11 @@
         new_small_accum_ref[:, at] = new_accum
 
 
-def update(targets, arrived, giant_weight, giant_accum, small_weight, small_accum, capacity, outer):
+def update(targets, arrived, giant_weight, giant_accum, small_weight, small_accum, capacity):
     giant_rows, width = giant_weight.shape
     small_rows = small_weight.shape[0]
     sources = targets.shape[1]
-    steps = 4
+    steps = 2
 
     def blocks(rows):
         return [pl.BlockSpec((rows // steps, width), lambda i: (i, 0)), pl.BlockSpec((1, rows // steps), lambda i: (0, i))]
@@ -245,7 +267,7 @@
         return [jax.ShapeDtypeStruct((rows, width), F32), jax.ShapeDtypeStruct((1, rows), F32)]
 
     return pl.pallas_call(
-        functools.partial(update_kernel, capacity, outer),
+        functools.partial(update_kernel, capacity),
         grid=(steps,),
         in_specs=[
             pl.BlockSpec((1, sources), lambda i: (0, 0)),
@@ -303,23 +325,29 @@
     samples = giant_slot.shape[2]
     exchange = functools.partial(lax.all_to_all, split_axis=0, concat_axis=0, tiled=True)
 
-    pairs = pooled_grad[0].reshape(-1, owners, 2, width)
-    small_values = exchange(pairs[:, :, 1, :].transpose(1, 0, 2), "col")
+    tables = pooled_grad[0].reshape(-1, owners, 2, width).transpose(1, 2, 0, 3)
+    small_values = exchange(tables[:, 1], "col")
     lengths = bag_lengths[0, 0]
     small_counts = bag_counts(masked_ids(small_ids[0, 0], lengths[:, 1]), small_weight.shape[1])
     giant_counts = bag_counts(masked_ids(giant_slot[0, 0], lengths[:, 0]), groups * capacity)
-    giant_out = after(pairs[:, :, 0, :].transpose(1, 0, 2), small_values, small_counts, giant_counts)
+    giant_out = after(tables, small_counts, giant_counts)[:, 0]
     giant_values = exchange(giant_out, "col").reshape(samples, width)
 
-    pieces = split_bucket_sums(small_counts, small_values.reshape(samples, width), position("rep"), lax.axis_size("rep"))
-    small_sum = sum(moved(piece, "rep", step) if step else piece for step, piece in enumerate(pieces))
-    terms = [moved(small_sum, "row", step) if step else small_sum for step in range(lax.axis_size("row"))]
-
-    packed = packed_bucket_sums(giant_counts, giant_values, capacity, position("row"), terms)
+    small_values = small_values.reshape(samples, width)
+    pieces = split_bucket_sums(small_counts, small_values, position("row"), lax.axis_size("row"))
+    terms = [moved(piece, "row", step) if step else piece for step, piece in enumerate(pieces)]
+    size = lax.axis_size("rep")
+    distance = size // 2
+    while distance:
+        keep, send = split_halves(terms, position("rep"), distance)
+        terms = [keep, lax.ppermute(send, "rep", [(i, i ^ distance) for i in range(size)])]
+        distance //= 2
+
+    packed = packed_bucket_sums(giant_counts, giant_values, capacity, terms)
     arrived = exchange(packed, ("row", "rep"))
     targets = touched_rows[0, :, 0, :].reshape(1, -1)
     new_gw, new_ga, new_sw, new_sa = update(
-        targets, arrived, giant_weight[0], giant_accum, small_weight[0], small_accum, capacity, len(terms)
+        targets, arrived, giant_weight[0], giant_accum, small_weight[0], small_accum, capacity
     )
     return (new_gw[None], new_ga, new_sw[None], new_sa)
 

time: 212 us -> 208 us (0.981)
  starting transfers between devices: 68.2 us -> 55 us
  waiting for transfers between devices: 74.5 us -> 83.1 us
    ppermute x10 -> x3, starting transfers between devices: 39.6 us -> 11.4 us  [moved(): lax.ppermute(value, axis, [(i, (i + step) % size) for i in range(size)])]
    ppermute x0 -> x3, starting transfers between devices: none -> 13.1 us  [body(): lax.ppermute(send, 'rep', [(i, i ^ distance) for i in range(size)])]
    all_to_all x1, waiting for transfers between devices: 0.01 us -> 11.1 us  [body(): giant_values = exchange(giant_out, 'col').reshape(samples, width)]
    ppermute x0 -> x3, waiting for transfers between devices: none -> 9.13 us  [body(): lax.ppermute(send, 'rep', [(i, i ^ distance) for i in range(size)])]
    ppermute x10 -> x3, waiting for transfers between devices: 16.6 us -> 8.37 us  [moved(): lax.ppermute(value, axis, [(i, (i + step) % size) for i in range(size)])]
    squeeze x0 -> x2, local copies, waits for them, and re-layouts: none -> 4.09 us  [the longest x1 2.75 us: body(): giant_out = after(tables, small_counts, giant_counts)[:, 0]]
    all_to_all x1, waiting for transfers between devices: 17.7 us -> 14.3 us  [body(): small_values = exchange(tables[:, 1], 'col')]
    pallas_call x1, Pallas kernels: 2.05 us -> 4.34 us  [split_bucket_sums(): pl.pallas_call(split_kernel, grid=(buckets // rows,), in_specs=[pl.BlockS...]
  transfers between devices with their start and end apart: 13 -> 9, of which waited for: 8 -> 8; matrix products, arithmetic and copies ran while one was open for 1% -> 2% of each run, Pallas kernels for 19% -> 21%
where the time goes in v4:
time: 208 us
  waiting for transfers between devices  83.1 us (40%)
  Pallas kernels  57.8 us (28%)
  starting transfers between devices  55 us (26%)
  local copies, waits for them, and re-layouts  10.2 us (5%)
    all_to_all x1, waiting for transfers between devices, body(): arrived = exchange(packed, ('row', 'rep'))  40.2 us
    pallas_call x2, Pallas kernels, bag_counts(): pl.pallas_call(counts_kernel, grid=(buckets // rows,), in_specs=[pl.Block...  38.2 us
    all_to_all x1, starting transfers between devices, body(): small_values = exchange(tables[:, 1], 'col')  15.5 us
    all_to_all x1, waiting for transfers between devices, body(): small_values = exchange(tables[:, 1], 'col')  14.3 us
    ppermute x3, starting transfers between devices, body(): lax.ppermute(send, 'rep', [(i, i ^ distance) for i in range(size)])  13.1 us
    ppermute x3, starting transfers between devices, moved(): lax.ppermute(value, axis, [(i, (i + step) % size) for i in range(size)])  11.4 us
    all_to_all x1, waiting for transfers between devices, body(): giant_values = exchange(giant_out, 'col').reshape(samples, width)  11.1 us
    all_to_all x1, starting transfers between devices, body(): arrived = exchange(packed, ('row', 'rep'))  10.3 us
  transfers between devices with their start and end apart: 9, of which 8 were waited for; matrix products, arithmetic and copies ran while one was open for 2% of the time, Pallas kernels for 21%

profile of v4, /device:TPU:8, one launch (start us, length us, event | category | flops | bytes accessed | tf_op | source)
XLA Modules:
  0.0 207.7 jit_solution(7145723588559809814)
XLA Ops:
  0.6 3.0 %copy.14 = bf16[1,128,48,256]{3,1,2,0:T(8,128)(2,1)S(1)} copy(bf16[1,128,48,256]{3,2,1,0:T(8,128)(2,1)} %param.9) | data formatting | bytes 6291456 | tf_op args[0]
  3.6 0.0 copy-start.6
  3.6 1.3 slice_bitcast_fusion
  5.0 0.0 copy-start.9
  5.0 0.0 copy-start.7
  5.0 0.8 copy-done.6
  5.8 15.5 %all-to-all-start.1 = ((bf16[24,128,256]{2,1,0:T(8,128)(2,1)}), bf16[24,128,256]{2,1,0:T(8,128)(2,1)}, u32[]{:S(2)}, u32[]{:S(2)}) async-start(bf16[24,128,256]{2,1,0:T(8,128)(2,1)} %slice_bitcast_fusion), calls=%async_computation.1 | async-start | bytes 3145728 | tf_op jit(solution)/shard_map/all_to_all | solution.py:329
  21.2 0.0 copy-done.9
  21.3 0.0 copy-done.7
  21.3 0.0 copy-start.8
  21.3 12.4 %shard_map.121.refs_1_.counts_ref = s8[1024,3072]{1,0:T(32,128)(4,1)S(1)} custom-call(s32[8,3072]{1,0:T(8,128)S(1)} %fusion.ids_ref), custom_call_target="tpu_custom_call" | custom-call | flops 75497472 | bytes 3145728 | tf_op jit(solution)/shard_map/pallas_call | solution.py:47
  33.7 0.0 copy-start
  33.7 1.7 copy-done
  35.5 0.0 copy-done.8
  35.5 25.7 %shard_map.120.refs_2_.counts_ref = s8[2048,3072]{1,0:T(32,128)(4,1)} custom-call(s32[8,3072]{1,0:T(8,128)S(1)} %fusion.1.ids_ref), custom_call_target="tpu_custom_call" | custom-call | flops 150994944 | bytes 6291456 | tf_op jit(solution)/shard_map/pallas_call | solution.py:47
  61.2 0.7 shard_map.122
  61.9 2.7 %slice_bitcast_fusion.1 = bf16[24,128,256]{2,1,0:T(8,128)(2,1)} fusion(bf16[24,2,128,256]{3,2,1,0:T(8,128)(2,1)} %shard_map.122), kind=kLoop, calls=%fused_computation.1 | loop fusion | bytes 3145728 | tf_op jit(solution)/shard_map/squeeze | solution.py:333
  64.7 0.0 copy-start.1
  64.7 14.3 %all-to-all-done.1 = bf16[24,128,256]{2,1,0:T(8,128)(2,1)} async-done(((bf16[24,128,256]{2,1,0:T(8,128)(2,1)}), bf16[24,128,256]{2,1,0:T(8,128)(2,1)}, u32[]{:S(2)}, u32[]{:S(2)}) %all-to-all-start.1) | async-done | bytes 1572896 | tf_op jit(solution)/shard_map/all_to_all | solution.py:329
  79.0 4.7 %all-to-all-start = ((bf16[24,128,256]{2,1,0:T(8,128)(2,1)}), bf16[24,128,256]{2,1,0:T(8,128)(2,1)}, u32[]{:S(2)}, u32[]{:S(2)}) async-start(bf16[24,128,256]{2,1,0:T(8,128)(2,1)} %slice_bitcast_fusion.1), calls=%async_computation | async-start | bytes 3145728 | tf_op jit(solution)/shard_map/all_to_all | solution.py:334
  83.7 0.0 copy-done.1
  83.7 4.3 %shard_map.123 = (f32[256,256]{1,0:T(8,128)S(1)}, f32[256,256]{1,0:T(8,128)}, f32[256,256]{1,0:T(8,128)}, f32[256,256]{1,0:T(8,128)}) custom-call(s32[1]{0:T(128)} %bitcast.12.place_ref, s8[1024,3072]{1,0:T(32,128)(4,1)S(1)} %copy-done.1, bf16[3072,256]{1,0:T(8,128)(2,1)} %bitcast.15.values_ref), custom_call_target="tpu_custom_call" | custom-call | tf_op jit(solution)/shard_map/pallas_call | solution.py:130
  88.0 3.4 %collective-permute-start = (f32[256,256]{1,0:T(8,128)}, f32[256,256]{1,0:T(8,128)S(1)}, u32[]{:S(2)}, u32[]{:S(2)}) collective-permute-start(f32[256,256]{1,0:T(8,128)} %get-tuple-element.19), channel_id=1, source_target_pairs={{0,8},{8,16},{16,24},{24,0},{1,9},{9,17},{17,25},{25,1},{2,10},{10... | collective-permute-start | bytes 786440 | tf_op jit(solution)/shard_map/ppermute | solution.py:303
  91.4 4.6 %collective-permute-start.1 = (f32[256,256]{1,0:T(8,128)}, f32[256,256]{1,0:T(8,128)S(1)}, u32[]{:S(2)}, u32[]{:S(2)}) collective-permute-start(f32[256,256]{1,0:T(8,128)} %get-tuple-element.20), channel_id=1, source_target_pairs={{0,16},{8,24},{16,0},{24,8},{1,17},{9,25},{17,1},{25,9},{2,18},{10... | collective-permute-start | bytes 786440 | tf_op jit(solution)/shard_map/ppermute | solution.py:303
  96.1 3.3 %collective-permute-start.2 = (f32[256,256]{1,0:T(8,128)}, f32[256,256]{1,0:T(8,128)S(1)}, u32[]{:S(2)}, u32[]{:S(2)}) collective-permute-start(f32[256,256]{1,0:T(8,128)} %get-tuple-element.21), channel_id=1, source_target_pairs={{0,24},{8,0},{16,8},{24,16},{1,25},{9,1},{17,9},{25,17},{2,26},{10... | collective-permute-start | bytes 786440 | tf_op jit(solution)/shard_map/ppermute | solution.py:303
  99.4 0.3 collective-permute-done.refs_1_
  99.7 6.6 %collective-permute-done.1.refs_2_ = f32[256,256]{1,0:T(8,128)S(1)} collective-permute-done((f32[256,256]{1,0:T(8,128)}, f32[256,256]{1,0:T(8,128)S(1)}, u32[]{:S(2)}, u32[]{:S(2)}) %collective-permute-start.1) | collective-permute-done | bytes 262176 | tf_op jit(solution)/shard_map/ppermute | solution.py:303
  106.3 1.5 collective-permute-done.2.refs_3_
  107.8 0.1 shard_map.124
  107.9 6.8 %collective-permute-start.3 = (f32[128,256]{1,0:T(8,128)S(1)}, f32[128,256]{1,0:T(8,128)S(1)}, u32[]{:S(2)}, u32[]{:S(2)}) collective-permute-start(f32[128,256]{1,0:T(8,128)S(1)} %get-tuple-element.23), channel_id=1, source_target_pairs={{0,4},{1,5},{2,6},{3,7},{4,0},{5,1},{6,2},{7,3},{8,12},{9,13},{10,... | collective-permute-start | bytes 393224 | tf_op jit(solution)/shard_map/ppermute | solution.py:343
  114.7 6.1 %collective-permute-done.3.refs_1_ = f32[128,256]{1,0:T(8,128)S(1)} collective-permute-done((f32[128,256]{1,0:T(8,128)S(1)}, f32[128,256]{1,0:T(8,128)S(1)}, u32[]{:S(2)}, u32[]{:S(2)}) %collective-permute-start.3) | collective-permute-done | bytes 131104 | tf_op jit(solution)/shard_map/ppermute | solution.py:343
  120.9 4.0 %collective-permute-start.4 = (f32[64,256]{1,0:T(8,128)S(1)}, f32[64,256]{1,0:T(8,128)S(1)}, u32[]{:S(2)}, u32[]{:S(2)}) collective-permute-start(f32[64,256]{1,0:T(8,128)S(1)} %get-tuple-element.25), channel_id=1, source_target_pairs={{0,2},{1,3},{2,0},{3,1},{4,6},{5,7},{6,4},{7,5},{8,10},{9,11},{10,... | collective-permute-start | bytes 196616 | tf_op jit(solution)/shard_map/ppermute | solution.py:343
  124.9 3.0 %collective-permute-done.4.refs_1_ = f32[64,256]{1,0:T(8,128)S(1)} collective-permute-done((f32[64,256]{1,0:T(8,128)S(1)}, f32[64,256]{1,0:T(8,128)S(1)}, u32[]{:S(2)}, u32[]{:S(2)}) %collective-permute-start.4) | collective-permute-done | bytes 65568 | tf_op jit(solution)/shard_map/ppermute | solution.py:343
  127.9 2.2 %collective-permute-start.5 = (f32[32,256]{1,0:T(8,128)S(1)}, f32[32,256]{1,0:T(8,128)S(1)}, u32[]{:S(2)}, u32[]{:S(2)}) collective-permute-start(f32[32,256]{1,0:T(8,128)S(1)} %get-tuple-element.27), channel_id=1, source_target_pairs={{0,1},{1,0},{2,3},{3,2},{4,5},{5,4},{6,7},{7,6},{8,9},{9,8},{10,11... | collective-permute-start | bytes 98312 | tf_op jit(solution)/shard_map/ppermute | solution.py:343
  130.2 11.1 %all-to-all-done = bf16[24,128,256]{2,1,0:T(8,128)(2,1)} async-done(((bf16[24,128,256]{2,1,0:T(8,128)(2,1)}), bf16[24,128,256]{2,1,0:T(8,128)(2,1)}, u32[]{:S(2)}, u32[]{:S(2)}) %all-to-all-start) | async-done | bytes 1572896 | tf_op jit(solution)/shard_map/all_to_all | solution.py:334
  141.3 0.0 collective-permute-done.5.refs_1_
  141.3 8.6 %shard_map.127 = s16[32,208,128]{2,1,0:T(8,128)(2,1)} custom-call(s8[2048,3072]{1,0:T(32,128)(4,1)} %shard_map.120.refs_2_.counts_ref, bf16[3072,256]{1,0:T(8,128)(2,1)} %bitcast.10.values_ref, f32[32,256]{1,0:T(8,128)S(1)} %get-tuple-element.26.refs_0_, f32[32,256]{1,0:T(8,128)S(1)} %collective-permute-done.5.refs_1_), custom_call_target="tpu_custom_call" | custom-call | tf_op jit(solution)/shard_map/pallas_call | solution.py:165
  150.0 0.0 copy-start.10
  150.0 0.0 copy-start.2
  150.0 0.0 copy-start.3
  150.0 0.0 copy-start.4
  150.0 0.0 copy-start.5
  150.0 10.3 %all-to-all-start.2 = ((s16[32,208,128]{2,1,0:T(8,128)(2,1)}), s16[32,208,128]{2,1,0:T(8,128)(2,1)S(1)}, u32[]{:S(2)}, u32[]{:S(2)}) async-start(s16[32,208,128]{2,1,0:T(8,128)(2,1)} %shard_map.127), calls=%async_computation.2 | async-start | bytes 3407872 | tf_op jit(solution)/shard_map/all_to_all | solution.py:347
  160.3 0.5 broadcast.3
  160.8 0.0 copy-done.10
  160.8 0.7 reduce.3
  161.5 0.1 reshape_squeeze.6.targets_ref
  161.6 40.2 %all-to-all-done.2.arrived_ref = s16[32,208,128]{2,1,0:T(8,128)(2,1)S(1)} async-done(((s16[32,208,128]{2,1,0:T(8,128)(2,1)}), s16[32,208,128]{2,1,0:T(8,128)(2,1)S(1)}, u32[]{:S(2)}, u32[]{:S(2)}) %all-to-all-start.2) | async-done | bytes 1703968 | tf_op jit(solution)/shard_map/all_to_all | solution.py:347
  201.8 0.0 copy-done.2
  201.8 0.0 copy-done.3
  201.8 0.0 copy-done.4
  201.8 0.0 copy-done.5
  201.8 5.9 %shard_map.128 = (f32[512,256]{1,0:T(8,128)}, f32[1,512]{1,0:T(1,128)}, f32[1024,256]{1,0:T(8,128)}, f32[1,1024]{1,0:T(1,128)}) custom-call(s32[1,2048]{1,0:T(1,128)S(1)} %reshape_squeeze.6.targets_ref, s16[32,208,128]{2,1,0:T(8,128)(2,1)S(1)} %all-to-all-done.2.arrived_ref, f32[512,256]{1,0:T(8,128)S(1)} %bitcast.31, f32[1,512]{1,0:T(1,128)S(1)} %copy-done.5, ...), custom_call_target="tpu_custom_call" | custom-call | tf_op jit(solution)/shard_map/pallas_call | solution.py:269
  (5 shorter events, 0.1 us)
Async XLA Ops:
  3.6 2.1 %copy-start.6 = (bf16[1,128,48,256]{3,1,2,0:T(8,128)(2,1)}, bf16[1,128,48,256]{3,1,2,0:T(8,128)(2,1)S(1)}, u32[]{:S(2)}) copy-start(bf16[1,128,48,256]{3,1,2,0:T(8,128)(2,1)S(1)} %copy.14) | copy-start | bytes 9437188
  5.0 16.3 %copy-start.9 = (s32[1,1,3072,2]{2,3,1,0:T(2,128)S(1)}, s32[1,1,3072,2]{2,3,1,0:T(2,128)}, u32[]{:S(2)}) copy-start(s32[1,1,3072,2]{2,3,1,0:T(2,128)} %param.12) | copy-start | bytes 73732
  5.0 16.3 %copy-start.7 = (s32[1,1,3072,8]{2,3,1,0:T(8,128)S(1)}, s32[1,1,3072,8]{2,3,1,0:T(8,128)}, u32[]{:S(2)}) copy-start(s32[1,1,3072,8]{2,3,1,0:T(8,128)} %param.13) | copy-start | bytes 294916
  5.8 73.2 %all-to-all-start.1 = ((bf16[24,128,256]{2,1,0:T(8,128)(2,1)}), bf16[24,128,256]{2,1,0:T(8,128)(2,1)}, u32[]{:S(2)}, u32[]{:S(2)}) async-start(bf16[24,128,256]{2,1,0:T(8,128)(2,1)} %slice_bitcast_fusion), calls=%async_computation.1 | async-start | bytes 3145728 | tf_op jit(solution)/shard_map/all_to_all | solution.py:329
  21.3 14.2 %copy-start.8 = (s32[1,1,3072,8]{2,3,1,0:T(8,128)S(1)}, s32[1,1,3072,8]{2,3,1,0:T(8,128)}, u32[]{:S(2)}) copy-start(s32[1,1,3072,8]{2,3,1,0:T(8,128)} %param.10) | copy-start | bytes 294916
  33.7 1.7 copy-start
  64.7 19.0 %copy-start.1 = (s8[1024,3072]{1,0:T(32,128)(4,1)S(1)}, s8[1024,3072]{1,0:T(32,128)(4,1)}, u32[]{:S(2)}) copy-start(s8[1024,3072]{1,0:T(32,128)(4,1)} %copy-done) | copy-start | bytes 9437188
  79.0 62.4 %all-to-all-start = ((bf16[24,128,256]{2,1,0:T(8,128)(2,1)}), bf16[24,128,256]{2,1,0:T(8,128)(2,1)}, u32[]{:S(2)}, u32[]{:S(2)}) async-start(bf16[24,128,256]{2,1,0:T(8,128)(2,1)} %slice_bitcast_fusion.1), calls=%async_computation | async-start | bytes 3145728 | tf_op jit(solution)/shard_map/all_to_all | solution.py:334
  88.0 11.7 %collective-permute-start = (f32[256,256]{1,0:T(8,128)}, f32[256,256]{1,0:T(8,128)S(1)}, u32[]{:S(2)}, u32[]{:S(2)}) collective-permute-start(f32[256,256]{1,0:T(8,128)} %get-tuple-element.19), channel_id=1, source_target_pairs={{0,8},{8,16},{16,24},{24,0},{1,9},{9,17},{17,25},{25,1},{2,10},{10... | collective-permute-start | bytes 786440 | tf_op jit(solution)/shard_map/ppermute | solution.py:303
  91.4 14.9 %collective-permute-start.1 = (f32[256,256]{1,0:T(8,128)}, f32[256,256]{1,0:T(8,128)S(1)}, u32[]{:S(2)}, u32[]{:S(2)}) collective-permute-start(f32[256,256]{1,0:T(8,128)} %get-tuple-element.20), channel_id=1, source_target_pairs={{0,16},{8,24},{16,0},{24,8},{1,17},{9,25},{17,1},{25,9},{2,18},{10... | collective-permute-start | bytes 786440 | tf_op jit(solution)/shard_map/ppermute | solution.py:303
  96.1 11.7 %collective-permute-start.2 = (f32[256,256]{1,0:T(8,128)}, f32[256,256]{1,0:T(8,128)S(1)}, u32[]{:S(2)}, u32[]{:S(2)}) collective-permute-start(f32[256,256]{1,0:T(8,128)} %get-tuple-element.21), channel_id=1, source_target_pairs={{0,24},{8,0},{16,8},{24,16},{1,25},{9,1},{17,9},{25,17},{2,26},{10... | collective-permute-start | bytes 786440 | tf_op jit(solution)/shard_map/ppermute | solution.py:303
  107.9 13.0 %collective-permute-start.3 = (f32[128,256]{1,0:T(8,128)S(1)}, f32[128,256]{1,0:T(8,128)S(1)}, u32[]{:S(2)}, u32[]{:S(2)}) collective-permute-start(f32[128,256]{1,0:T(8,128)S(1)} %get-tuple-element.23), channel_id=1, source_target_pairs={{0,4},{1,5},{2,6},{3,7},{4,0},{5,1},{6,2},{7,3},{8,12},{9,13},{10,... | collective-permute-start | bytes 393224 | tf_op jit(solution)/shard_map/ppermute | solution.py:343
  120.9 7.1 %collective-permute-start.4 = (f32[64,256]{1,0:T(8,128)S(1)}, f32[64,256]{1,0:T(8,128)S(1)}, u32[]{:S(2)}, u32[]{:S(2)}) collective-permute-start(f32[64,256]{1,0:T(8,128)S(1)} %get-tuple-element.25), channel_id=1, source_target_pairs={{0,2},{1,3},{2,0},{3,1},{4,6},{5,7},{6,4},{7,5},{8,10},{9,11},{10,... | collective-permute-start | bytes 196616 | tf_op jit(solution)/shard_map/ppermute | solution.py:343
  127.9 13.4 %collective-permute-start.5 = (f32[32,256]{1,0:T(8,128)S(1)}, f32[32,256]{1,0:T(8,128)S(1)}, u32[]{:S(2)}, u32[]{:S(2)}) collective-permute-start(f32[32,256]{1,0:T(8,128)S(1)} %get-tuple-element.27), channel_id=1, source_target_pairs={{0,1},{1,0},{2,3},{3,2},{4,5},{5,4},{6,7},{7,6},{8,9},{9,8},{10,11... | collective-permute-start | bytes 98312 | tf_op jit(solution)/shard_map/ppermute | solution.py:343
  150.0 10.9 %copy-start.10 = (s32[1,32,1,64]{3,2,1,0:T(1,128)S(1)}, s32[1,32,1,64]{3,2,1,0:T(1,128)}, u32[]{:S(2)}) copy-start(s32[1,32,1,64]{3,2,1,0:T(1,128)} %param.11) | copy-start | bytes 24580
  150.0 51.8 %copy-start.2 = (f32[1,1024,256]{2,1,0:T(8,128)S(1)}, f32[1,1024,256]{2,1,0:T(8,128)}, u32[]{:S(2)}) copy-start(f32[1,1024,256]{2,1,0:T(8,128)} %param.16) | copy-start | bytes 3145732
  150.0 51.8 %copy-start.3 = (f32[1,512,256]{2,1,0:T(8,128)S(1)}, f32[1,512,256]{2,1,0:T(8,128)}, u32[]{:S(2)}) copy-start(f32[1,512,256]{2,1,0:T(8,128)} %param.14) | copy-start | bytes 1572868
  150.0 51.8 %copy-start.4 = (f32[1,1024]{1,0:T(1,128)S(1)}, f32[1,1024]{1,0:T(1,128)}, u32[]{:S(2)}) copy-start(f32[1,1024]{1,0:T(1,128)} %small_accum_ref.1) | copy-start | bytes 12292
  150.0 51.8 %copy-start.5 = (f32[1,512]{1,0:T(1,128)S(1)}, f32[1,512]{1,0:T(1,128)}, u32[]{:S(2)}) copy-start(f32[1,512]{1,0:T(1,128)} %giant_accum_ref.1) | copy-start | bytes 6148
  150.0 51.8 %all-to-all-start.2 = ((s16[32,208,128]{2,1,0:T(8,128)(2,1)}), s16[32,208,128]{2,1,0:T(8,128)(2,1)S(1)}, u32[]{:S(2)}, u32[]{:S(2)}) async-start(s16[32,208,128]{2,1,0:T(8,128)(2,1)} %shard_map.127), calls=%async_computation.2 | async-start | bytes 3407872 | tf_op jit(solution)/shard_map/all_to_all | solution.py:347

commit v5 on v4

--- a/solution.py
+++ b/solution.py
@@ -97,28 +97,35 @@
 
 
 def packed_kernel(capacity, counts_ref, values_ref, *refs):
-    terms, out_ref = refs[:-1], refs[-1]
+    terms, (out_ref, small_coded, small_tag) = refs[:-3], refs[-3:]
+    lanes = out_ref.shape[2]
+    mine, width = small_coded.shape
+
+    def along_lanes(power, first):
+        shape = (power.shape[0], lanes)
+        row = lax.broadcasted_iota(jnp.int32, shape, 0) + first
+        spread = jnp.where(row == lax.broadcasted_iota(jnp.int32, shape, 1), jnp.broadcast_to(power, shape), 0.0)
+        return jnp.broadcast_to(jnp.sum(spread, axis=0, keepdims=True), (TAG_ROWS, lanes))
+
+    @pl.when(pl.program_id(0) == 0)
+    def _():
+        small = terms[0][...]
+        for term in terms[1:]:
+            small = small + term[...]
+        coded, power = coded_rows(small)
+        small_coded[...] = coded
+        small_tag[...] = along_lanes(power, capacity)
+
     sums = jnp.dot(counts_ref[...].astype(BF), values_ref[...], preferred_element_type=F32)
     coded, power = coded_rows(sums)
-    rows, width = sums.shape
-    lanes = out_ref.shape[2]
-    mine = terms[0].shape[0]
-    small = terms[0][...]
-    for term in terms[1:]:
-        small = small + term[...]
-    small_coded, small_power = coded_rows(small)
-    tall = capacity + mine
-    diagonal = lax.broadcasted_iota(jnp.int32, (tall, lanes), 0) == lax.broadcasted_iota(jnp.int32, (tall, lanes), 1)
-    for block in range(rows // capacity):
+    for block in range(sums.shape[0] // capacity):
         slots = slice(block * capacity, (block + 1) * capacity)
         first = 0
-        for piece, count in ((coded[slots, :], capacity), (small_coded, mine)):
+        for piece, count in ((coded[slots, :], capacity), (small_coded[...], mine)):
             for part in range(width // lanes):
                 out_ref[block, first : first + count, :] = piece[:, part * lanes : (part + 1) * lanes]
                 first += count
-        powers = jnp.concatenate([power[slots, :], small_power], axis=0)
-        spread = jnp.where(diagonal, jnp.broadcast_to(powers, (tall, lanes)), 0.0)
-        tag = jnp.broadcast_to(jnp.sum(spread, axis=0, keepdims=True), (TAG_ROWS, lanes))
+        tag = along_lanes(power[slots, :], 0) + small_tag[...]
         out_ref[block, first:, :] = tag.astype(jnp.int32).astype(jnp.int16)
 
 
@@ -172,6 +179,7 @@
         + [whole] * len(terms),
         out_specs=pl.BlockSpec((rows // capacity, tall, lanes), lambda i: (i, 0, 0)),
         out_shape=jax.ShapeDtypeStruct((buckets // capacity, tall, lanes), jnp.int16),
+        scratch_shapes=[pltpu.VMEM((mine, width), jnp.int16), pltpu.VMEM((TAG_ROWS, lanes), F32)],
         compiler_params=pltpu.CompilerParams(vmem_limit_bytes=VMEM_LIMIT),
     )(counts, values, *terms)
 

time: 208 us -> 208 us (level)
  no operation moved by 1% of the time
where the time goes in v5:
time: 208 us; the launch traced here: 207 us
  waiting for transfers between devices  83.1 us (40%)
  Pallas kernels  57 us (27%)
  starting transfers between devices  55 us (26%)
  local copies, waits for them, and re-layouts  10.2 us (5%)
    all_to_all x1, waiting for transfers between devices, body(): arrived = exchange(packed, ('row', 'rep'))  40.2 us
    pallas_call x2, Pallas kernels, bag_counts(): pl.pallas_call(counts_kernel, grid=(buckets // rows,), in_specs=[pl.Block...  38.2 us
    all_to_all x1, starting transfers between devices, body(): small_values = exchange(tables[:, 1], 'col')  15.5 us
    all_to_all x1, waiting for transfers between devices, body(): small_values = exchange(tables[:, 1], 'col')  14.3 us
    ppermute x3, starting transfers between devices, body(): lax.ppermute(send, 'rep', [(i, i ^ distance) for i in range(size)])  13.1 us
    ppermute x3, starting transfers between devices, moved(): lax.ppermute(value, axis, [(i, (i + step) % size) for i in range(size)])  11.4 us
    all_to_all x1, waiting for transfers between devices, body(): giant_values = exchange(giant_out, 'col').reshape(samples, width)  11.1 us
    all_to_all x1, starting transfers between devices, body(): arrived = exchange(packed, ('row', 'rep'))  10.3 us
  transfers between devices with their start and end apart: 9, of which 8 were waited for; matrix products, arithmetic and copies ran while one was open for 2% of the time, Pallas kernels for 21%

profile of v5, /device:TPU:8, one launch (start us, length us, event | category | flops | bytes accessed | tf_op | source)
XLA Modules:
  0.0 206.9 jit_solution(12215454768264249746)
XLA Ops:
  0.6 3.0 %copy.14 = bf16[1,128,48,256]{3,1,2,0:T(8,128)(2,1)S(1)} copy(bf16[1,128,48,256]{3,2,1,0:T(8,128)(2,1)} %param.9) | data formatting | bytes 6291456 | tf_op args[0]
  3.6 0.0 copy-start.6
  3.6 1.3 slice_bitcast_fusion
  5.0 0.0 copy-start.9
  5.0 0.0 copy-start.7
  5.0 0.8 copy-done.6
  5.8 15.5 %all-to-all-start.1 = ((bf16[24,128,256]{2,1,0:T(8,128)(2,1)}), bf16[24,128,256]{2,1,0:T(8,128)(2,1)}, u32[]{:S(2)}, u32[]{:S(2)}) async-start(bf16[24,128,256]{2,1,0:T(8,128)(2,1)} %slice_bitcast_fusion), calls=%async_computation.1 | async-start | bytes 3145728 | tf_op jit(solution)/shard_map/all_to_all | solution.py:337
  21.2 0.0 copy-done.9
  21.3 0.0 copy-done.7
  21.3 0.0 copy-start.8
  21.3 12.4 %shard_map.121.refs_1_.counts_ref = s8[1024,3072]{1,0:T(32,128)(4,1)S(1)} custom-call(s32[8,3072]{1,0:T(8,128)S(1)} %fusion.ids_ref), custom_call_target="tpu_custom_call" | custom-call | flops 75497472 | bytes 3145728 | tf_op jit(solution)/shard_map/pallas_call | solution.py:47
  33.7 0.0 copy-start
  33.7 1.7 copy-done
  35.5 0.0 copy-done.8
  35.5 25.7 %shard_map.120.refs_2_.counts_ref = s8[2048,3072]{1,0:T(32,128)(4,1)} custom-call(s32[8,3072]{1,0:T(8,128)S(1)} %fusion.1.ids_ref), custom_call_target="tpu_custom_call" | custom-call | flops 150994944 | bytes 6291456 | tf_op jit(solution)/shard_map/pallas_call | solution.py:47
  61.2 0.7 shard_map.122
  61.9 2.7 %slice_bitcast_fusion.1 = bf16[24,128,256]{2,1,0:T(8,128)(2,1)} fusion(bf16[24,2,128,256]{3,2,1,0:T(8,128)(2,1)} %shard_map.122), kind=kLoop, calls=%fused_computation.1 | loop fusion | bytes 3145728 | tf_op jit(solution)/shard_map/squeeze | solution.py:341
  64.7 0.0 copy-start.1
  64.7 14.3 %all-to-all-done.1 = bf16[24,128,256]{2,1,0:T(8,128)(2,1)} async-done(((bf16[24,128,256]{2,1,0:T(8,128)(2,1)}), bf16[24,128,256]{2,1,0:T(8,128)(2,1)}, u32[]{:S(2)}, u32[]{:S(2)}) %all-to-all-start.1) | async-done | bytes 1572896 | tf_op jit(solution)/shard_map/all_to_all | solution.py:337
  79.0 4.7 %all-to-all-start = ((bf16[24,128,256]{2,1,0:T(8,128)(2,1)}), bf16[24,128,256]{2,1,0:T(8,128)(2,1)}, u32[]{:S(2)}, u32[]{:S(2)}) async-start(bf16[24,128,256]{2,1,0:T(8,128)(2,1)} %slice_bitcast_fusion.1), calls=%async_computation | async-start | bytes 3145728 | tf_op jit(solution)/shard_map/all_to_all | solution.py:342
  83.7 0.0 copy-done.1
  83.7 4.3 %shard_map.123 = (f32[256,256]{1,0:T(8,128)S(1)}, f32[256,256]{1,0:T(8,128)}, f32[256,256]{1,0:T(8,128)}, f32[256,256]{1,0:T(8,128)}) custom-call(s32[1]{0:T(128)} %bitcast.12.place_ref, s8[1024,3072]{1,0:T(32,128)(4,1)S(1)} %copy-done.1, bf16[3072,256]{1,0:T(8,128)(2,1)} %bitcast.15.values_ref), custom_call_target="tpu_custom_call" | custom-call | tf_op jit(solution)/shard_map/pallas_call | solution.py:137
  88.0 3.4 %collective-permute-start = (f32[256,256]{1,0:T(8,128)}, f32[256,256]{1,0:T(8,128)S(1)}, u32[]{:S(2)}, u32[]{:S(2)}) collective-permute-start(f32[256,256]{1,0:T(8,128)} %get-tuple-element.19), channel_id=1, source_target_pairs={{0,8},{8,16},{16,24},{24,0},{1,9},{9,17},{17,25},{25,1},{2,10},{10... | collective-permute-start | bytes 786440 | tf_op jit(solution)/shard_map/ppermute | solution.py:311
  91.4 4.6 %collective-permute-start.1 = (f32[256,256]{1,0:T(8,128)}, f32[256,256]{1,0:T(8,128)S(1)}, u32[]{:S(2)}, u32[]{:S(2)}) collective-permute-start(f32[256,256]{1,0:T(8,128)} %get-tuple-element.20), channel_id=1, source_target_pairs={{0,16},{8,24},{16,0},{24,8},{1,17},{9,25},{17,1},{25,9},{2,18},{10... | collective-permute-start | bytes 786440 | tf_op jit(solution)/shard_map/ppermute | solution.py:311
  96.1 3.3 %collective-permute-start.2 = (f32[256,256]{1,0:T(8,128)}, f32[256,256]{1,0:T(8,128)S(1)}, u32[]{:S(2)}, u32[]{:S(2)}) collective-permute-start(f32[256,256]{1,0:T(8,128)} %get-tuple-element.21), channel_id=1, source_target_pairs={{0,24},{8,0},{16,8},{24,16},{1,25},{9,1},{17,9},{25,17},{2,26},{10... | collective-permute-start | bytes 786440 | tf_op jit(solution)/shard_map/ppermute | solution.py:311
  99.4 0.3 collective-permute-done.refs_1_
  99.7 6.6 %collective-permute-done.1.refs_2_ = f32[256,256]{1,0:T(8,128)S(1)} collective-permute-done((f32[256,256]{1,0:T(8,128)}, f32[256,256]{1,0:T(8,128)S(1)}, u32[]{:S(2)}, u32[]{:S(2)}) %collective-permute-start.1) | collective-permute-done | bytes 262176 | tf_op jit(solution)/shard_map/ppermute | solution.py:311
  106.3 1.5 collective-permute-done.2.refs_3_
  107.8 0.1 shard_map.124
  107.9 6.8 %collective-permute-start.3 = (f32[128,256]{1,0:T(8,128)S(1)}, f32[128,256]{1,0:T(8,128)S(1)}, u32[]{:S(2)}, u32[]{:S(2)}) collective-permute-start(f32[128,256]{1,0:T(8,128)S(1)} %get-tuple-element.23), channel_id=1, source_target_pairs={{0,4},{1,5},{2,6},{3,7},{4,0},{5,1},{6,2},{7,3},{8,12},{9,13},{10,... | collective-permute-start | bytes 393224 | tf_op jit(solution)/shard_map/ppermute | solution.py:351
  114.7 6.1 %collective-permute-done.3.refs_1_ = f32[128,256]{1,0:T(8,128)S(1)} collective-permute-done((f32[128,256]{1,0:T(8,128)S(1)}, f32[128,256]{1,0:T(8,128)S(1)}, u32[]{:S(2)}, u32[]{:S(2)}) %collective-permute-start.3) | collective-permute-done | bytes 131104 | tf_op jit(solution)/shard_map/ppermute | solution.py:351
  120.9 4.0 %collective-permute-start.4 = (f32[64,256]{1,0:T(8,128)S(1)}, f32[64,256]{1,0:T(8,128)S(1)}, u32[]{:S(2)}, u32[]{:S(2)}) collective-permute-start(f32[64,256]{1,0:T(8,128)S(1)} %get-tuple-element.25), channel_id=1, source_target_pairs={{0,2},{1,3},{2,0},{3,1},{4,6},{5,7},{6,4},{7,5},{8,10},{9,11},{10,... | collective-permute-start | bytes 196616 | tf_op jit(solution)/shard_map/ppermute | solution.py:351
  124.9 3.0 %collective-permute-done.4.refs_1_ = f32[64,256]{1,0:T(8,128)S(1)} collective-permute-done((f32[64,256]{1,0:T(8,128)S(1)}, f32[64,256]{1,0:T(8,128)S(1)}, u32[]{:S(2)}, u32[]{:S(2)}) %collective-permute-start.4) | collective-permute-done | bytes 65568 | tf_op jit(solution)/shard_map/ppermute | solution.py:351
  127.9 2.2 %collective-permute-start.5 = (f32[32,256]{1,0:T(8,128)S(1)}, f32[32,256]{1,0:T(8,128)S(1)}, u32[]{:S(2)}, u32[]{:S(2)}) collective-permute-start(f32[32,256]{1,0:T(8,128)S(1)} %get-tuple-element.27), channel_id=1, source_target_pairs={{0,1},{1,0},{2,3},{3,2},{4,5},{5,4},{6,7},{7,6},{8,9},{9,8},{10,11... | collective-permute-start | bytes 98312 | tf_op jit(solution)/shard_map/ppermute | solution.py:351
  130.2 11.1 %all-to-all-done = bf16[24,128,256]{2,1,0:T(8,128)(2,1)} async-done(((bf16[24,128,256]{2,1,0:T(8,128)(2,1)}), bf16[24,128,256]{2,1,0:T(8,128)(2,1)}, u32[]{:S(2)}, u32[]{:S(2)}) %all-to-all-start) | async-done | bytes 1572896 | tf_op jit(solution)/shard_map/all_to_all | solution.py:342
  141.3 0.0 collective-permute-done.5.refs_1_
  141.3 7.8 %shard_map.127 = s16[32,208,128]{2,1,0:T(8,128)(2,1)} custom-call(s8[2048,3072]{1,0:T(32,128)(4,1)} %shard_map.120.refs_2_.counts_ref, bf16[3072,256]{1,0:T(8,128)(2,1)} %bitcast.10.values_ref, f32[32,256]{1,0:T(8,128)S(1)} %get-tuple-element.26.refs_0_, f32[32,256]{1,0:T(8,128)S(1)} %collective-permute-done.5.refs_1_), custom_call_target="tpu_custom_call" | custom-call | tf_op jit(solution)/shard_map/pallas_call | solution.py:172
  149.2 0.0 copy-start.10
  149.2 0.0 copy-start.2
  149.2 0.0 copy-start.3
  149.2 0.0 copy-start.4
  149.2 0.0 copy-start.5
  149.2 10.3 %all-to-all-start.2 = ((s16[32,208,128]{2,1,0:T(8,128)(2,1)}), s16[32,208,128]{2,1,0:T(8,128)(2,1)S(1)}, u32[]{:S(2)}, u32[]{:S(2)}) async-start(s16[32,208,128]{2,1,0:T(8,128)(2,1)} %shard_map.127), calls=%async_computation.2 | async-start | bytes 3407872 | tf_op jit(solution)/shard_map/all_to_all | solution.py:355
  159.5 0.5 broadcast.3
  160.0 0.0 copy-done.10
  160.0 0.7 reduce.3
  160.7 0.1 reshape_squeeze.6.targets_ref
  160.8 40.2 %all-to-all-done.2.arrived_ref = s16[32,208,128]{2,1,0:T(8,128)(2,1)S(1)} async-done(((s16[32,208,128]{2,1,0:T(8,128)(2,1)}), s16[32,208,128]{2,1,0:T(8,128)(2,1)S(1)}, u32[]{:S(2)}, u32[]{:S(2)}) %all-to-all-start.2) | async-done | bytes 1703968 | tf_op jit(solution)/shard_map/all_to_all | solution.py:355
  201.0 0.0 copy-done.2
  201.0 0.0 copy-done.3
  201.0 0.0 copy-done.4
  201.0 0.0 copy-done.5
  201.0 5.9 %shard_map.128 = (f32[512,256]{1,0:T(8,128)}, f32[1,512]{1,0:T(1,128)}, f32[1024,256]{1,0:T(8,128)}, f32[1,1024]{1,0:T(1,128)}) custom-call(s32[1,2048]{1,0:T(1,128)S(1)} %reshape_squeeze.6.targets_ref, s16[32,208,128]{2,1,0:T(8,128)(2,1)S(1)} %all-to-all-done.2.arrived_ref, f32[512,256]{1,0:T(8,128)S(1)} %bitcast.31, f32[1,512]{1,0:T(1,128)S(1)} %copy-done.5, ...), custom_call_target="tpu_custom_call" | custom-call | tf_op jit(solution)/shard_map/pallas_call | solution.py:277
  (5 shorter events, 0.1 us)
Async XLA Ops:
  3.6 2.1 %copy-start.6 = (bf16[1,128,48,256]{3,1,2,0:T(8,128)(2,1)}, bf16[1,128,48,256]{3,1,2,0:T(8,128)(2,1)S(1)}, u32[]{:S(2)}) copy-start(bf16[1,128,48,256]{3,1,2,0:T(8,128)(2,1)S(1)} %copy.14) | copy-start | bytes 9437188
  5.0 16.3 %copy-start.9 = (s32[1,1,3072,2]{2,3,1,0:T(2,128)S(1)}, s32[1,1,3072,2]{2,3,1,0:T(2,128)}, u32[]{:S(2)}) copy-start(s32[1,1,3072,2]{2,3,1,0:T(2,128)} %param.12) | copy-start | bytes 73732
  5.0 16.3 %copy-start.7 = (s32[1,1,3072,8]{2,3,1,0:T(8,128)S(1)}, s32[1,1,3072,8]{2,3,1,0:T(8,128)}, u32[]{:S(2)}) copy-start(s32[1,1,3072,8]{2,3,1,0:T(8,128)} %param.13) | copy-start | bytes 294916
  5.8 73.2 %all-to-all-start.1 = ((bf16[24,128,256]{2,1,0:T(8,128)(2,1)}), bf16[24,128,256]{2,1,0:T(8,128)(2,1)}, u32[]{:S(2)}, u32[]{:S(2)}) async-start(bf16[24,128,256]{2,1,0:T(8,128)(2,1)} %slice_bitcast_fusion), calls=%async_computation.1 | async-start | bytes 3145728 | tf_op jit(solution)/shard_map/all_to_all | solution.py:337
  21.3 14.2 %copy-start.8 = (s32[1,1,3072,8]{2,3,1,0:T(8,128)S(1)}, s32[1,1,3072,8]{2,3,1,0:T(8,128)}, u32[]{:S(2)}) copy-start(s32[1,1,3072,8]{2,3,1,0:T(8,128)} %param.10) | copy-start | bytes 294916
  33.7 1.7 copy-start
  64.7 19.0 %copy-start.1 = (s8[1024,3072]{1,0:T(32,128)(4,1)S(1)}, s8[1024,3072]{1,0:T(32,128)(4,1)}, u32[]{:S(2)}) copy-start(s8[1024,3072]{1,0:T(32,128)(4,1)} %copy-done) | copy-start | bytes 9437188
  79.0 62.4 %all-to-all-start = ((bf16[24,128,256]{2,1,0:T(8,128)(2,1)}), bf16[24,128,256]{2,1,0:T(8,128)(2,1)}, u32[]{:S(2)}, u32[]{:S(2)}) async-start(bf16[24,128,256]{2,1,0:T(8,128)(2,1)} %slice_bitcast_fusion.1), calls=%async_computation | async-start | bytes 3145728 | tf_op jit(solution)/shard_map/all_to_all | solution.py:342
  88.0 11.7 %collective-permute-start = (f32[256,256]{1,0:T(8,128)}, f32[256,256]{1,0:T(8,128)S(1)}, u32[]{:S(2)}, u32[]{:S(2)}) collective-permute-start(f32[256,256]{1,0:T(8,128)} %get-tuple-element.19), channel_id=1, source_target_pairs={{0,8},{8,16},{16,24},{24,0},{1,9},{9,17},{17,25},{25,1},{2,10},{10... | collective-permute-start | bytes 786440 | tf_op jit(solution)/shard_map/ppermute | solution.py:311
  91.4 14.9 %collective-permute-start.1 = (f32[256,256]{1,0:T(8,128)}, f32[256,256]{1,0:T(8,128)S(1)}, u32[]{:S(2)}, u32[]{:S(2)}) collective-permute-start(f32[256,256]{1,0:T(8,128)} %get-tuple-element.20), channel_id=1, source_target_pairs={{0,16},{8,24},{16,0},{24,8},{1,17},{9,25},{17,1},{25,9},{2,18},{10... | collective-permute-start | bytes 786440 | tf_op jit(solution)/shard_map/ppermute | solution.py:311
  96.1 11.7 %collective-permute-start.2 = (f32[256,256]{1,0:T(8,128)}, f32[256,256]{1,0:T(8,128)S(1)}, u32[]{:S(2)}, u32[]{:S(2)}) collective-permute-start(f32[256,256]{1,0:T(8,128)} %get-tuple-element.21), channel_id=1, source_target_pairs={{0,24},{8,0},{16,8},{24,16},{1,25},{9,1},{17,9},{25,17},{2,26},{10... | collective-permute-start | bytes 786440 | tf_op jit(solution)/shard_map/ppermute | solution.py:311
  107.9 13.0 %collective-permute-start.3 = (f32[128,256]{1,0:T(8,128)S(1)}, f32[128,256]{1,0:T(8,128)S(1)}, u32[]{:S(2)}, u32[]{:S(2)}) collective-permute-start(f32[128,256]{1,0:T(8,128)S(1)} %get-tuple-element.23), channel_id=1, source_target_pairs={{0,4},{1,5},{2,6},{3,7},{4,0},{5,1},{6,2},{7,3},{8,12},{9,13},{10,... | collective-permute-start | bytes 393224 | tf_op jit(solution)/shard_map/ppermute | solution.py:351
  120.9 7.1 %collective-permute-start.4 = (f32[64,256]{1,0:T(8,128)S(1)}, f32[64,256]{1,0:T(8,128)S(1)}, u32[]{:S(2)}, u32[]{:S(2)}) collective-permute-start(f32[64,256]{1,0:T(8,128)S(1)} %get-tuple-element.25), channel_id=1, source_target_pairs={{0,2},{1,3},{2,0},{3,1},{4,6},{5,7},{6,4},{7,5},{8,10},{9,11},{10,... | collective-permute-start | bytes 196616 | tf_op jit(solution)/shard_map/ppermute | solution.py:351
  127.9 13.4 %collective-permute-start.5 = (f32[32,256]{1,0:T(8,128)S(1)}, f32[32,256]{1,0:T(8,128)S(1)}, u32[]{:S(2)}, u32[]{:S(2)}) collective-permute-start(f32[32,256]{1,0:T(8,128)S(1)} %get-tuple-element.27), channel_id=1, source_target_pairs={{0,1},{1,0},{2,3},{3,2},{4,5},{5,4},{6,7},{7,6},{8,9},{9,8},{10,11... | collective-permute-start | bytes 98312 | tf_op jit(solution)/shard_map/ppermute | solution.py:351
  149.2 10.9 %copy-start.10 = (s32[1,32,1,64]{3,2,1,0:T(1,128)S(1)}, s32[1,32,1,64]{3,2,1,0:T(1,128)}, u32[]{:S(2)}) copy-start(s32[1,32,1,64]{3,2,1,0:T(1,128)} %param.11) | copy-start | bytes 24580
  149.2 51.8 %copy-start.2 = (f32[1,1024,256]{2,1,0:T(8,128)S(1)}, f32[1,1024,256]{2,1,0:T(8,128)}, u32[]{:S(2)}) copy-start(f32[1,1024,256]{2,1,0:T(8,128)} %param.16) | copy-start | bytes 3145732
  149.2 51.8 %copy-start.3 = (f32[1,512,256]{2,1,0:T(8,128)S(1)}, f32[1,512,256]{2,1,0:T(8,128)}, u32[]{:S(2)}) copy-start(f32[1,512,256]{2,1,0:T(8,128)} %param.14) | copy-start | bytes 1572868
  149.2 51.8 %copy-start.4 = (f32[1,1024]{1,0:T(1,128)S(1)}, f32[1,1024]{1,0:T(1,128)}, u32[]{:S(2)}) copy-start(f32[1,1024]{1,0:T(1,128)} %small_accum_ref.1) | copy-start | bytes 12292
  149.2 51.8 %copy-start.5 = (f32[1,512]{1,0:T(1,128)S(1)}, f32[1,512]{1,0:T(1,128)}, u32[]{:S(2)}) copy-start(f32[1,512]{1,0:T(1,128)} %giant_accum_ref.1) | copy-start | bytes 6148
  149.2 51.8 %all-to-all-start.2 = ((s16[32,208,128]{2,1,0:T(8,128)(2,1)}), s16[32,208,128]{2,1,0:T(8,128)(2,1)S(1)}, u32[]{:S(2)}, u32[]{:S(2)}) async-start(s16[32,208,128]{2,1,0:T(8,128)(2,1)} %shard_map.127), calls=%async_computation.2 | async-start | bytes 3407872 | tf_op jit(solution)/shard_map/all_to_all | solution.py:355
